TPU v7x, 128 devices: a whole 4x4x4 slice. The times are simulated.
128 devices in a mesh: curve: 32 (over x, z, core), sub: 4 (over y).
Axes of the slice: x: 4, y: 4, z: 4, core: 2. Of those that a mesh axis runs over, the one named last changes fastest.
Arguments:
- child_poles: bfloat16 [8, 64, 262144], P(None, None, ('curve', 'sub')), may hold values from -6 to 6
- m2m_ops: bfloat16 [8, 64, 64], replicated, may hold values from -0.25 to 0.25
- m2l_ops: bfloat16 [316, 64, 64], replicated, may hold values from -0.078125 to 0.078125
- near_partner: int32 [88, 262144], P(None, ('curve', 'sub')), may hold values from -1 to 2047, as said below
- near_op: int32 [88], replicated, may hold values from 0 to 315, as said below
- far_source: int32 [128, 128, 128], P(('curve', 'sub')), may hold values from -1 to 2047, as said below
- far_target: int32 [128, 128, 128], P(('curve', 'sub')), may hold values from -1 to 2047, as said below
- far_op: int32 [128], replicated, may hold values from 0 to 315, as said below
Outputs:
- child_locals: bfloat16 [8, 64, 262144], P(None, None, ('curve', 'sub'))
Inputs may be any that keep to these rules, and one draw needn't show every extreme that they name: `near_partner`: -1 marks an empty slot; otherwise the index, among the 2048 boxes of the box's own device, of a box later on the curve. `near_op`: distinct operator indices. `far_op`: distinct operator indices. `far_source`: entry [d, q, c] is -1 exactly where far_target[d, q, c] is -1 (an empty slot), always where q = d; otherwise an index among the boxes of device d. The used slots of each [d, q] come first; for every d some q has all 128 slots used. `far_target`: entry [d, q, c] is -1 exactly where far_source[d, q, c] is -1; otherwise an index among the boxes of device q.
All inputs are finite; a program needn't handle non-finite values.
Results may differ from a plain program's by a relative error of at most 0.0065.
Values may be sent and summed in bfloat16 or wider, within the bound.
No kernel may reach another device: no remote copies, remote signals or barrier semaphores. Data moves between devices by JAX's collectives and lax.ppermute only.
A program may use at most 128 MiB of HBM per device.

v0:
```python
import jax
import jax.numpy as jnp
from jax import lax
from jax.sharding import PartitionSpec as P


def on_device(child_poles, m2m_ops, m2l_ops, near_partner, near_op, far_source, far_target, far_op):
    rank = m2m_ops.shape[1]
    boxes = child_poles.shape[2]
    poles = jnp.einsum(
        "cij,cjb->ib", m2m_ops, child_poles, preferred_element_type=jnp.float32
    ).astype(jnp.bfloat16)
    groups = near_partner.shape[0] // 8
    partner_blocks = near_partner.reshape(groups, 8, boxes)
    op_blocks = m2l_ops[near_op].reshape(groups, 8, rank, rank)

    def near_step(local, block):
        partner, operators = block
        valid = partner >= 0
        index = jnp.maximum(partner, 0)
        fetched = jnp.take(poles, index, axis=1)
        fetched = jnp.where(valid[None], fetched, jnp.zeros((), jnp.bfloat16))
        local = local + jnp.einsum(
            "jik,kjb->ib", operators, fetched, preferred_element_type=jnp.float32
        )
        back = jnp.einsum("jki,kb->ijb", operators, poles, preferred_element_type=jnp.float32)
        back = jnp.where(valid[None], back, 0.0)
        local = local.at[:, index.reshape(-1)].add(back.reshape(rank, -1))
        return (local, None)

    local, _ = lax.scan(
        near_step, jnp.zeros((rank, boxes), jnp.float32), (partner_blocks, op_blocks)
    )
    far_ops = m2l_ops[far_op]
    source = far_source[0]
    target = far_target[0]
    valid = source >= 0
    source_index = jnp.maximum(source, 0)
    own = jnp.take(poles, source_index, axis=1)
    own = jnp.where(valid[None], own, jnp.zeros((), jnp.bfloat16))
    asked = lax.all_to_all(target, ("curve", "sub"), split_axis=0, concat_axis=0, tiled=True)
    asked_valid = asked >= 0
    asked_index = jnp.maximum(asked, 0)
    served = jnp.take(poles, asked_index, axis=1)
    fetched = lax.all_to_all(served, ("curve", "sub"), split_axis=1, concat_axis=1, tiled=True)
    ahead = jnp.einsum("cik,kpc->ipc", far_ops, fetched, preferred_element_type=jnp.float32)
    ahead = jnp.where(valid[None], ahead, 0.0)
    local = local.at[:, source_index.reshape(-1)].add(ahead.reshape(rank, -1))
    partial_value = jnp.einsum("cki,kpc->ipc", far_ops, own, preferred_element_type=jnp.float32)
    partial_value = lax.all_to_all(
        partial_value, ("curve", "sub"), split_axis=1, concat_axis=1, tiled=True
    )
    partial_value = jnp.where(asked_valid[None], partial_value, 0.0)
    local = local.at[:, asked_index.reshape(-1)].add(partial_value.reshape(rank, -1))
    rounded_local = local.astype(jnp.bfloat16)
    return jnp.einsum(
        "cji,jb->cib", m2m_ops, rounded_local, preferred_element_type=jnp.float32
    ).astype(jnp.bfloat16)


def solution(mesh):
    placed = (
        P(None, None, ("curve", "sub")),
        P(),
        P(),
        P(None, ("curve", "sub")),
        P(),
        P(("curve", "sub"), None, None),
        P(("curve", "sub"), None, None),
        P(),
    )
    return jax.shard_map(
        on_device,
        mesh=mesh,
        in_specs=placed,
        out_specs=P(None, None, ("curve", "sub")),
        check_vma=False,
    )
```

profile of v0, /device:TPU:1, one launch (start us, length us, event | category | flops | bytes accessed | tf_op | source)
XLA Modules:
  0.0 2309.5 jit_solution(4511042129354130831)
XLA Ops:
  198.9 1845.2 %while.10 = (s32[]{:T(128)}, f32[64,2048]{0,1:T(8,128)S(1)}, bf16[11,8,64,64]{3,2,1,0:T(8,128)(2,1)}, s32[11,8,2048]{2,1,0:T(8,128)}, bf16[64,2048]{0,1:T(8,128)(2,1)S(1)}, /*index=5*/s32[]{:T(128)}) while((s32[]{:T(128)}, f32[64,2048]{0,1:T(8,128)S(1)}, bf16[11,8,64,64]{3,2,1,0:T(8,128)(2,1)}, s32[11,8,2048]{2,1,0:T(8,128)}, ...), condition=%wide.region_2.3_spmd, body=%wide.region_0.2_spmd.sunk | while | flops 272842752 | bytes 48382044 | solution.py:31
  276.9 89.8 %scatter_fusion = f32[64,2048]{0,1:T(8,128)S(1)} fusion(f32[64,2048]{0,1:T(8,128)S(1)} %copy.191, s32[16384]{0:T(1024)S(1)} %bitcast.130, f32[16384,64]{1,0:T(8,128)} %copy.193), kind=kCustom, calls=%fused_computation.5.clone.1 | custom fusion | flops 1048576 | bytes 12648448 | tf_op jit(solution)/shard_map/while/body/eval_jaxpr/scatter-add | solution.py:28
  367.9 57.8 %gather_fusion = bf16[16384,64]{1,0:T(8,128)(2,1)} fusion(bf16[64,2048]{0,1:T(8,128)(2,1)S(1)} %get-tuple-element.127, s32[16384]{0:T(1024)S(1)} %broadcast_clamp_fusion.2), kind=kCustom, calls=%fused_computation.clone.1 | custom fusion | bytes 4259840 | tf_op jit(solution)/shard_map/while/body/eval_jaxpr/jit(_take)/gather | solution.py:21
  444.7 89.6 %scatter_fusion = f32[64,2048]{0,1:T(8,128)S(1)} fusion(f32[64,2048]{0,1:T(8,128)S(1)} %copy.191, s32[16384]{0:T(1024)S(1)} %bitcast.130, f32[16384,64]{1,0:T(8,128)} %copy.193), kind=kCustom, calls=%fused_computation.5.clone.1 | custom fusion | flops 1048576 | bytes 12648448 | tf_op jit(solution)/shard_map/while/body/eval_jaxpr/scatter-add | solution.py:28
  535.6 57.8 %gather_fusion = bf16[16384,64]{1,0:T(8,128)(2,1)} fusion(bf16[64,2048]{0,1:T(8,128)(2,1)S(1)} %get-tuple-element.127, s32[16384]{0:T(1024)S(1)} %broadcast_clamp_fusion.2), kind=kCustom, calls=%fused_computation.clone.1 | custom fusion | bytes 4259840 | tf_op jit(solution)/shard_map/while/body/eval_jaxpr/jit(_take)/gather | solution.py:21
  612.4 89.8 %scatter_fusion = f32[64,2048]{0,1:T(8,128)S(1)} fusion(f32[64,2048]{0,1:T(8,128)S(1)} %copy.191, s32[16384]{0:T(1024)S(1)} %bitcast.130, f32[16384,64]{1,0:T(8,128)} %copy.193), kind=kCustom, calls=%fused_computation.5.clone.1 | custom fusion | flops 1048576 | bytes 12648448 | tf_op jit(solution)/shard_map/while/body/eval_jaxpr/scatter-add | solution.py:28
  703.4 57.8 %gather_fusion = bf16[16384,64]{1,0:T(8,128)(2,1)} fusion(bf16[64,2048]{0,1:T(8,128)(2,1)S(1)} %get-tuple-element.127, s32[16384]{0:T(1024)S(1)} %broadcast_clamp_fusion.2), kind=kCustom, calls=%fused_computation.clone.1 | custom fusion | bytes 4259840 | tf_op jit(solution)/shard_map/while/body/eval_jaxpr/jit(_take)/gather | solution.py:21
  780.2 89.6 %scatter_fusion = f32[64,2048]{0,1:T(8,128)S(1)} fusion(f32[64,2048]{0,1:T(8,128)S(1)} %copy.191, s32[16384]{0:T(1024)S(1)} %bitcast.130, f32[16384,64]{1,0:T(8,128)} %copy.193), kind=kCustom, calls=%fused_computation.5.clone.1 | custom fusion | flops 1048576 | bytes 12648448 | tf_op jit(solution)/shard_map/while/body/eval_jaxpr/scatter-add | solution.py:28
  871.1 57.8 %gather_fusion = bf16[16384,64]{1,0:T(8,128)(2,1)} fusion(bf16[64,2048]{0,1:T(8,128)(2,1)S(1)} %get-tuple-element.127, s32[16384]{0:T(1024)S(1)} %broadcast_clamp_fusion.2), kind=kCustom, calls=%fused_computation.clone.1 | custom fusion | bytes 4259840 | tf_op jit(solution)/shard_map/while/body/eval_jaxpr/jit(_take)/gather | solution.py:21
  947.9 89.8 %scatter_fusion = f32[64,2048]{0,1:T(8,128)S(1)} fusion(f32[64,2048]{0,1:T(8,128)S(1)} %copy.191, s32[16384]{0:T(1024)S(1)} %bitcast.130, f32[16384,64]{1,0:T(8,128)} %copy.193), kind=kCustom, calls=%fused_computation.5.clone.1 | custom fusion | flops 1048576 | bytes 12648448 | tf_op jit(solution)/shard_map/while/body/eval_jaxpr/scatter-add | solution.py:28
  1038.8 57.8 %gather_fusion = bf16[16384,64]{1,0:T(8,128)(2,1)} fusion(bf16[64,2048]{0,1:T(8,128)(2,1)S(1)} %get-tuple-element.127, s32[16384]{0:T(1024)S(1)} %broadcast_clamp_fusion.2), kind=kCustom, calls=%fused_computation.clone.1 | custom fusion | bytes 4259840 | tf_op jit(solution)/shard_map/while/body/eval_jaxpr/jit(_take)/gather | solution.py:21
  1115.6 89.7 %scatter_fusion = f32[64,2048]{0,1:T(8,128)S(1)} fusion(f32[64,2048]{0,1:T(8,128)S(1)} %copy.191, s32[16384]{0:T(1024)S(1)} %bitcast.130, f32[16384,64]{1,0:T(8,128)} %copy.193), kind=kCustom, calls=%fused_computation.5.clone.1 | custom fusion | flops 1048576 | bytes 12648448 | tf_op jit(solution)/shard_map/while/body/eval_jaxpr/scatter-add | solution.py:28
  1206.5 57.8 %gather_fusion = bf16[16384,64]{1,0:T(8,128)(2,1)} fusion(bf16[64,2048]{0,1:T(8,128)(2,1)S(1)} %get-tuple-element.127, s32[16384]{0:T(1024)S(1)} %broadcast_clamp_fusion.2), kind=kCustom, calls=%fused_computation.clone.1 | custom fusion | bytes 4259840 | tf_op jit(solution)/shard_map/while/body/eval_jaxpr/jit(_take)/gather | solution.py:21
  1283.3 89.6 %scatter_fusion = f32[64,2048]{0,1:T(8,128)S(1)} fusion(f32[64,2048]{0,1:T(8,128)S(1)} %copy.191, s32[16384]{0:T(1024)S(1)} %bitcast.130, f32[16384,64]{1,0:T(8,128)} %copy.193), kind=kCustom, calls=%fused_computation.5.clone.1 | custom fusion | flops 1048576 | bytes 12648448 | tf_op jit(solution)/shard_map/while/body/eval_jaxpr/scatter-add | solution.py:28
  1374.1 57.8 %gather_fusion = bf16[16384,64]{1,0:T(8,128)(2,1)} fusion(bf16[64,2048]{0,1:T(8,128)(2,1)S(1)} %get-tuple-element.127, s32[16384]{0:T(1024)S(1)} %broadcast_clamp_fusion.2), kind=kCustom, calls=%fused_computation.clone.1 | custom fusion | bytes 4259840 | tf_op jit(solution)/shard_map/while/body/eval_jaxpr/jit(_take)/gather | solution.py:21
  1450.9 89.9 %scatter_fusion = f32[64,2048]{0,1:T(8,128)S(1)} fusion(f32[64,2048]{0,1:T(8,128)S(1)} %copy.191, s32[16384]{0:T(1024)S(1)} %bitcast.130, f32[16384,64]{1,0:T(8,128)} %copy.193), kind=kCustom, calls=%fused_computation.5.clone.1 | custom fusion | flops 1048576 | bytes 12648448 | tf_op jit(solution)/shard_map/while/body/eval_jaxpr/scatter-add | solution.py:28
  1542.0 57.8 %gather_fusion = bf16[16384,64]{1,0:T(8,128)(2,1)} fusion(bf16[64,2048]{0,1:T(8,128)(2,1)S(1)} %get-tuple-element.127, s32[16384]{0:T(1024)S(1)} %broadcast_clamp_fusion.2), kind=kCustom, calls=%fused_computation.clone.1 | custom fusion | bytes 4259840 | tf_op jit(solution)/shard_map/while/body/eval_jaxpr/jit(_take)/gather | solution.py:21
  1618.8 89.7 %scatter_fusion = f32[64,2048]{0,1:T(8,128)S(1)} fusion(f32[64,2048]{0,1:T(8,128)S(1)} %copy.191, s32[16384]{0:T(1024)S(1)} %bitcast.130, f32[16384,64]{1,0:T(8,128)} %copy.193), kind=kCustom, calls=%fused_computation.5.clone.1 | custom fusion | flops 1048576 | bytes 12648448 | tf_op jit(solution)/shard_map/while/body/eval_jaxpr/scatter-add | solution.py:28
  1709.8 57.8 %gather_fusion = bf16[16384,64]{1,0:T(8,128)(2,1)} fusion(bf16[64,2048]{0,1:T(8,128)(2,1)S(1)} %get-tuple-element.127, s32[16384]{0:T(1024)S(1)} %broadcast_clamp_fusion.2), kind=kCustom, calls=%fused_computation.clone.1 | custom fusion | bytes 4259840 | tf_op jit(solution)/shard_map/while/body/eval_jaxpr/jit(_take)/gather | solution.py:21
  1786.6 89.6 %scatter_fusion = f32[64,2048]{0,1:T(8,128)S(1)} fusion(f32[64,2048]{0,1:T(8,128)S(1)} %copy.191, s32[16384]{0:T(1024)S(1)} %bitcast.130, f32[16384,64]{1,0:T(8,128)} %copy.193), kind=kCustom, calls=%fused_computation.5.clone.1 | custom fusion | flops 1048576 | bytes 12648448 | tf_op jit(solution)/shard_map/while/body/eval_jaxpr/scatter-add | solution.py:28
  1877.5 57.8 %gather_fusion = bf16[16384,64]{1,0:T(8,128)(2,1)} fusion(bf16[64,2048]{0,1:T(8,128)(2,1)S(1)} %get-tuple-element.127, s32[16384]{0:T(1024)S(1)} %broadcast_clamp_fusion.2), kind=kCustom, calls=%fused_computation.clone.1 | custom fusion | bytes 4259840 | tf_op jit(solution)/shard_map/while/body/eval_jaxpr/jit(_take)/gather | solution.py:21
  1954.2 89.8 %scatter_fusion = f32[64,2048]{0,1:T(8,128)S(1)} fusion(f32[64,2048]{0,1:T(8,128)S(1)} %copy.191, s32[16384]{0:T(1024)S(1)} %bitcast.130, f32[16384,64]{1,0:T(8,128)} %copy.193), kind=kCustom, calls=%fused_computation.5.clone.1 | custom fusion | flops 1048576 | bytes 12648448 | tf_op jit(solution)/shard_map/while/body/eval_jaxpr/scatter-add | solution.py:28
  2072.8 103.4 %scatter_fusion.1 = f32[64,2048]{0,1:T(8,128)S(1)} fusion(f32[64,2048]{0,1:T(8,128)S(1)} %get-tuple-element.33, s32[16384]{0:T(1024)S(1)} %maximum_bitcast_fusion.2, f32[16384,64]{1,0:T(8,128)} %copy.155), kind=kCustom, calls=%fused_computation.6 | custom fusion | flops 1048576 | bytes 12648448 | tf_op jit(solution)/shard_map/scatter-add | solution.py:48
  2205.7 100.6 %scatter_fusion.2 = f32[64,2048]{0,1:T(8,128)S(1)} fusion(f32[64,2048]{0,1:T(8,128)S(1)} %scatter_fusion.1, s32[16384]{0:T(1024)S(1)} %maximum_bitcast_fusion.1, f32[16384,64]{1,0:T(8,128)} %copy.166), kind=kCustom, calls=%fused_computation.7 | custom fusion | flops 1048576 | bytes 12648448 | tf_op jit(solution)/shard_map/scatter-add | solution.py:54
  (193 shorter events, 539.9 us)
Async XLA Ops:
  0.0 11.5 copy-start
  0.0 21.3 all-to-all-start
  21.3 57.8 %copy-start.2 = (s32[128,1,128]{2,1,0:T(1,128)}, s32[128,1,128]{2,1,0:T(1,128)S(1)}, u32[]{:S(2)}) copy-start(s32[128,1,128]{2,1,0:T(1,128)S(1)} %all-to-all-done) | copy-start | bytes 196612
  89.2 99.2 %all-to-all-start.1 = ((bf16[64,128,128]{2,0,1:T(8,128)(2,1)}), bf16[64,128,128]{2,0,1:T(8,128)(2,1)}, u32[]{:S(2)}, u32[]{:S(2)}) async-start(bf16[64,128,128]{2,0,1:T(8,128)(2,1)} %copy.151), calls=%async_computation.1 | async-start | bytes 4194304 | tf_op jit(solution)/shard_map/all_to_all | solution.py:45
  94.1 10.1 copy-start.9
  104.2 4.4 copy-start.10
  108.6 4.6 copy-start.4
  113.4 64.5 %copy-start.7 = (pred[128,128]{0,1:T(8,128)(4,1)}, pred[128,128]{0,1:T(8,128)(4,1)S(1)}, u32[]{:S(2)}) copy-start(pred[128,128]{0,1:T(8,128)(4,1)S(1)} %copy.147) | copy-start | bytes 49156
  188.4 1987.8 %all-to-all-start.2 = ((f32[64,128,128]{2,0,1:T(8,128)}), f32[64,128,128]{2,0,1:T(8,128)}, u32[]{:S(2)}, u32[]{:S(2)}) async-start(f32[64,128,128]{2,0,1:T(8,128)} %copy.163), calls=%async_computation.2 | async-start | bytes 8388608 | tf_op jit(solution)/shard_map/all_to_all | solution.py:50
  198.9 1845.2 %copy-start.6 = (bf16[8,64,64]{2,1,0:T(8,128)(2,1)S(1)}, bf16[8,64,64]{2,1,0:T(8,128)(2,1)}, u32[]{:S(2)}) copy-start(bf16[8,64,64]{2,1,0:T(8,128)(2,1)} %param.13) | copy-start | bytes 196612
  198.9 1845.3 %copy-start.5 = (s32[1,128,128]{2,1,0:T(8,128)S(1)}, s32[1,128,128]{2,1,0:T(8,128)}, u32[]{:S(2)}) copy-start(s32[1,128,128]{2,1,0:T(8,128)} %param.17) | copy-start | bytes 196612
  198.9 1845.4 %copy-start.3 = (s32[128,1,128]{2,1,0:T(1,128)S(1)}, s32[128,1,128]{2,1,0:T(1,128)}, u32[]{:S(2)}) copy-start(s32[128,1,128]{2,1,0:T(1,128)} %copy-done.2) | copy-start | bytes 196612
  2044.4 4.6 copy-start.8
  2307.2 2.3 copy-start.1
where the time goes:
time: 2360 us; the launch traced here: 2310 us
  other arithmetic  1220 us (52%)
  local copies, waits for them, and re-layouts  1000 us (42%)
  matrix products  55 us (2%)
  starting transfers between devices  26.7 us (1%)
    scatter-add x11, other arithmetic, near_step(): local = local.at[:, index.reshape(-1)].add(back.reshape(rank, -1))  987 us
    gather x22, local copies, waits for them, and re-layouts, near_step(): fetched = jnp.take(poles, index, axis=1)  688 us
    scatter-add x1, other arithmetic, on_device(): local = local.at[:, source_index.reshape(-1)].add(ahead.reshape(rank, -1))  103 us
    scatter-add x1, other arithmetic, on_device(): local.at[:, asked_index.reshape(-1)].add(partial_value.reshape(rank, -1))  101 us
    reshape x22, local copies, waits for them, and re-layouts, near_step(): local = local.at[:, index.reshape(-1)].add(back.reshape(rank, -1))  100 us
    gather x2, local copies, waits for them, and re-layouts, on_device(): own = jnp.take(poles, source_index, axis=1)  64.3 us
    gather x2, local copies, waits for them, and re-layouts, on_device(): served = jnp.take(poles, asked_index, axis=1)  63.4 us
  transfers between devices with their start and end apart: 3, of which 1 were waited for; matrix products, arithmetic and copies ran while one was open for 90% of the time, Pallas kernels for 0%

commit v1 on v0

v1 whole, which is shorter than its diff:
```python
import functools

import jax
import jax.numpy as jnp
from jax import lax
from jax.experimental import pallas as pl
from jax.experimental.pallas import tpu as pltpu
from jax.sharding import PartitionSpec as P

RANK = 64
CHILD = 8
BOX = 2048
PEERS = 128
CAP = 128
PAIRS = 88
GROUPS = 4
LANES = 128
WIDE = GROUPS * RANK
TB = 512
NB = BOX // TB
WIDTH = [(BOX - b * TB) // GROUPS for b in range(NB)]
START = [sum(WIDTH[:b]) for b in range(NB)]
BATCH = 4
SPAN = BOX // GROUPS
QUAD = 4
EMPTY = 512
CENTRE = 256
SENT = RANK + 16
f32 = jnp.float32
bf16 = jnp.bfloat16
VMEM = pl.BlockSpec(memory_space=pltpu.VMEM)
SMEM = pl.BlockSpec(memory_space=pltpu.SMEM)
LIMIT = 56 * 2**20
NT = (((1,), (1,)), ((), ()))
TN = (((0,), (0,)), ((), ()))


def fill_table(table_ref):
    table_ref[...] = (lax.broadcasted_iota(jnp.int32, table_ref.shape, 0) - CENTRE).astype(f32).astype(bf16)


def split_index(rel, valid, width):
    group = ((rel >= width).astype(jnp.int32) + (rel >= 2 * width).astype(jnp.int32)
             + (rel >= 3 * width).astype(jnp.int32))
    place = jnp.where(valid, rel - group * width - CENTRE, EMPTY)
    return place.astype(f32), jnp.where(valid, group, 0).astype(f32)


def one_hot(table_ref, place, rows):
    n = place.shape[1]
    row = jnp.broadcast_to(place, (16, n)).astype(bf16)
    parts = []
    for r in range(rows // 16):
        here = table_ref[r * 16:(r + 1) * 16, :]
        here = jnp.concatenate([here] * (n // LANES), axis=1)
        parts.append(jnp.where(here == row, jnp.ones((), bf16), jnp.zeros((), bf16)))
    return jnp.concatenate(parts, axis=0)


def pick_group(stacked, group):
    out = stacked[0:RANK]
    for k in range(1, GROUPS):
        out = jnp.where(group == float(k), stacked[k * RANK:(k + 1) * RANK], out)
    return out


def spread_group(values, group):
    n = values.shape[1]
    row = jnp.broadcast_to(group, (16, n)).astype(bf16)
    parts = []
    for k in range(GROUPS):
        mask = row == jnp.array(k, bf16)
        parts += [jnp.where(mask, values[r * 16:(r + 1) * 16], jnp.zeros((), bf16)) for r in range(RANK // 16)]
    return jnp.concatenate(parts, axis=0)


def stack_groups(poles_ref, stack_ref):
    for k in range(GROUPS):
        stack_ref[k * RANK:(k + 1) * RANK, :] = poles_ref[:, k * SPAN:(k + 1) * SPAN]


def gather_quads(table_ref, stack_ref, place_ref, group_ref, hot_ref, store):
    def quad(n, _):
        place = jnp.concatenate([place_ref[pl.ds(n * QUAD + i, 1), :] for i in range(QUAD)], axis=1)
        group = jnp.concatenate([group_ref[pl.ds(n * QUAD + i, 1), :] for i in range(QUAD)], axis=1)
        hot_ref[...] = one_hot(table_ref, place, SPAN)
        found = jnp.dot(stack_ref[...], hot_ref[...], preferred_element_type=f32)
        found = pick_group(found, group).astype(bf16)
        for i in range(QUAD):
            store(n * QUAD + i, found[:, i * CAP:(i + 1) * CAP])
        return 0

    lax.fori_loop(0, PEERS // QUAD, quad, 0)


def up_kernel(child_ref, m2m_ref, source_ref, target_ref, poles_ref, send_ref,
              table_ref, stack_ref, place_ref, group_ref, ask_place_ref, ask_group_ref, hot_ref):
    fill_table(table_ref)
    ops = jnp.concatenate([m2m_ref[c] for c in range(CHILD)], axis=1)
    for s in range(0, BOX, 512):
        poles_ref[:, s:s + 512] = jnp.dot(
            ops, child_ref[:, s:s + 512], preferred_element_type=f32).astype(bf16)
    stack_groups(poles_ref, stack_ref)
    source = source_ref[...]
    place_ref[...], group_ref[...] = split_index(source, source >= 0, SPAN)
    target = target_ref[...]
    ask_place_ref[...], ask_group_ref[...] = split_index(target, target >= 0, SPAN)
    sub = lax.broadcasted_iota(jnp.int32, (16, CAP), 0)

    def store(q, block):
        send_ref[q, 0:RANK, :] = block
        ask = jnp.where(sub == 0, ask_place_ref[pl.ds(q, 1), :],
                        jnp.where(sub == 1, ask_group_ref[pl.ds(q, 1), :], 0.0))
        send_ref[q, RANK:SENT, :] = ask.astype(bf16)

    gather_quads(table_ref, stack_ref, place_ref, group_ref, hot_ref, store)


def upward(child, m2m, source, target):
    return pl.pallas_call(
        up_kernel,
        out_shape=(jax.ShapeDtypeStruct((RANK, BOX), bf16), jax.ShapeDtypeStruct((PEERS, SENT, CAP), bf16)),
        in_specs=[VMEM] * 4,
        out_specs=(VMEM, VMEM),
        scratch_shapes=[
            pltpu.VMEM((SPAN, LANES), bf16),
            pltpu.VMEM((WIDE, SPAN), bf16),
            pltpu.VMEM((PEERS, CAP), f32),
            pltpu.VMEM((PEERS, CAP), f32),
            pltpu.VMEM((PEERS, CAP), f32),
            pltpu.VMEM((PEERS, CAP), f32),
            pltpu.VMEM((SPAN, QUAD * CAP), bf16),
        ],
        compiler_params=pltpu.CompilerParams(vmem_limit_bytes=LIMIT),
        cost_estimate=pl.CostEstimate(flops=10**10, bytes_accessed=6 << 20, transcendentals=0),
        name="upward",
    )(child, m2m, source, target)


def serve_kernel(poles_ref, received_ref, out_ref, table_ref, stack_ref, place_ref, group_ref, hot_ref):
    fill_table(table_ref)
    stack_groups(poles_ref, stack_ref)

    def unpack(d, _):
        ask = received_ref[d, RANK:SENT, :].astype(f32)
        place_ref[pl.ds(d, 1), :] = ask[0:1]
        group_ref[pl.ds(d, 1), :] = ask[1:2]
        return 0

    lax.fori_loop(0, PEERS, unpack, 0)

    def store(d, block):
        out_ref[d, :, :] = block

    gather_quads(table_ref, stack_ref, place_ref, group_ref, hot_ref, store)


def serve(poles, received):
    return pl.pallas_call(
        serve_kernel,
        out_shape=jax.ShapeDtypeStruct((PEERS, RANK, CAP), bf16),
        in_specs=[VMEM] * 2,
        out_specs=VMEM,
        scratch_shapes=[
            pltpu.VMEM((SPAN, LANES), bf16),
            pltpu.VMEM((WIDE, SPAN), bf16),
            pltpu.VMEM((PEERS, CAP), f32),
            pltpu.VMEM((PEERS, CAP), f32),
            pltpu.VMEM((SPAN, QUAD * CAP), bf16),
        ],
        compiler_params=pltpu.CompilerParams(vmem_limit_bytes=LIMIT),
        cost_estimate=pl.CostEstimate(flops=10**10, bytes_accessed=4 << 20, transcendentals=0),
        name="serve",
    )(poles, received)


def near_kernel(first, batches, op_ref, poles_ref, partner_ref, m2l_ref, out_ref,
                table_ref, stack_ref, place_ref, group_ref, back_ref, ahead_ref, hot_ref, *totals):
    fill_table(table_ref)
    for b in range(NB):
        for k in range(GROUPS):
            s = b * TB + k * WIDTH[b]
            stack_ref[k * RANK:(k + 1) * RANK, START[b]:START[b] + WIDTH[b]] = poles_ref[:, s:s + WIDTH[b]]
        totals[b][...] = jnp.zeros(totals[b].shape, f32)
    slots = batches * BATCH
    for r in range(0, slots, 8):
        n = min(8, slots - r)
        for b in range(NB):
            block = slice(b * TB, (b + 1) * TB)
            partner = partner_ref[first + r:first + r + n, block]
            place, group = split_index(partner - b * TB, partner >= 0, WIDTH[b])
            place_ref[r:r + n, block] = place
            group_ref[r:r + n, block] = group
    out_ref[...] = jnp.zeros(out_ref.shape, f32)

    def batch(n, _):
        ops = jnp.concatenate([m2l_ref[op_ref[first + n * BATCH + j]] for j in range(BATCH)], axis=1)
        back_ref[...] = lax.dot_general(ops, poles_ref[...], TN, preferred_element_type=f32).astype(bf16)
        for j in range(BATCH):
            rows = slice(j * RANK, (j + 1) * RANK)
            for b in range(NB):
                block = slice(b * TB, (b + 1) * TB)
                width = WIDTH[b]
                place = place_ref[pl.ds(n * BATCH + j, 1), block]
                group = group_ref[pl.ds(n * BATCH + j, 1), block]
                side = (j * NB + b) % 2
                hot_ref[side, :width, :] = one_hot(table_ref, place, width)
                hot = hot_ref[side, :width, :]
                found = jnp.dot(stack_ref[:, START[b]:START[b] + width], hot, preferred_element_type=f32)
                ahead_ref[rows, block] = pick_group(found, group).astype(bf16)
                spread = spread_group(back_ref[rows, block], group)
                totals[b][...] += lax.dot_general(hot, spread, NT, preferred_element_type=f32)
        out_ref[...] += jnp.dot(ops, ahead_ref[...], preferred_element_type=f32)
        return 0

    lax.fori_loop(0, batches, batch, 0)
    for b in range(NB):
        for k in range(GROUPS):
            s = b * TB + k * WIDTH[b]
            out_ref[:, s:s + WIDTH[b]] += jnp.transpose(totals[b][...][:, k * RANK:(k + 1) * RANK])


def near(near_op, poles, partner, m2l, first, batches):
    return pl.pallas_call(
        functools.partial(near_kernel, first, batches),
        out_shape=jax.ShapeDtypeStruct((RANK, BOX), f32),
        in_specs=[SMEM, VMEM, VMEM, VMEM],
        out_specs=VMEM,
        scratch_shapes=[
            pltpu.VMEM((LANES * 4, LANES), bf16),
            pltpu.VMEM((WIDE, sum(WIDTH)), bf16),
            pltpu.VMEM((batches * BATCH, BOX), f32),
            pltpu.VMEM((batches * BATCH, BOX), f32),
            pltpu.VMEM((BATCH * RANK, BOX), bf16),
            pltpu.VMEM((BATCH * RANK, BOX), bf16),
            pltpu.VMEM((2, WIDTH[0], TB), bf16),
        ] + [pltpu.VMEM((WIDTH[b], WIDE), f32) for b in range(NB)],
        compiler_params=pltpu.CompilerParams(vmem_limit_bytes=LIMIT),
        cost_estimate=pl.CostEstimate(flops=10**9 * batches * BATCH, bytes_accessed=6 << 20, transcendentals=0),
        name="near",
    )(near_op, poles, partner, m2l)


def down_kernel(op_ref, near_a_ref, near_b_ref, served_ref, own_ref, source_ref, m2l_ref, m2m_ref, out_ref,
                table_ref, place_ref, group_ref, hot_ref, spread_ref, total_ref, local_ref):
    fill_table(table_ref)
    source = source_ref[...]
    place, group = split_index(source, source >= 0, SPAN)
    place_ref[...] = jnp.transpose(place)
    group_ref[...] = jnp.transpose(group)
    total_ref[...] = jnp.zeros(total_ref.shape, f32)

    def quad(n, _):
        for side in range(2):
            values, places, groups = [], [], []
            for i in range(QUAD):
                c = n * QUAD + i
                op = m2l_ref[op_ref[c]]
                if side == 0:
                    value = jnp.dot(op, served_ref[c], preferred_element_type=f32)
                    places.append(place_ref[pl.ds(c, 1), :])
                    groups.append(group_ref[pl.ds(c, 1), :])
                else:
                    value = lax.dot_general(op, own_ref[c, 0:RANK, :], TN, preferred_element_type=f32)
                    ask = own_ref[c, RANK:SENT, :].astype(f32)
                    places.append(ask[0:1])
                    groups.append(ask[1:2])
                values.append(value.astype(bf16))
            lanes = slice(side * QUAD * PEERS, (side + 1) * QUAD * PEERS)
            hot_ref[:, lanes] = one_hot(table_ref, jnp.concatenate(places, axis=1), SPAN)
            spread_ref[:, lanes] = spread_group(jnp.concatenate(values, axis=1), jnp.concatenate(groups, axis=1))
        total_ref[...] += lax.dot_general(hot_ref[...], spread_ref[...], NT, preferred_element_type=f32)
        return 0

    lax.fori_loop(0, CAP // QUAD, quad, 0)
    for k in range(GROUPS):
        cols = slice(k * SPAN, (k + 1) * SPAN)
        far = jnp.transpose(total_ref[...][:, k * RANK:(k + 1) * RANK])
        local_ref[:, cols] = (near_a_ref[:, cols] + near_b_ref[:, cols] + far).astype(bf16)
    ops = jnp.concatenate([m2m_ref[c] for c in range(CHILD)], axis=1)
    for s in range(0, BOX, 256):
        out_ref[:, s:s + 256] = lax.dot_general(
            ops, local_ref[:, s:s + 256], TN, preferred_element_type=f32).astype(bf16)


def downward(far_op, near_a, near_b, served, own, source, m2l, m2m):
    return pl.pallas_call(
        down_kernel,
        out_shape=jax.ShapeDtypeStruct((CHILD * RANK, BOX), bf16),
        in_specs=[SMEM] + [VMEM] * 7,
        out_specs=VMEM,
        scratch_shapes=[
            pltpu.VMEM((SPAN, LANES), bf16),
            pltpu.VMEM((CAP, PEERS), f32),
            pltpu.VMEM((CAP, PEERS), f32),
            pltpu.VMEM((SPAN, 2 * QUAD * PEERS), bf16),
            pltpu.VMEM((WIDE, 2 * QUAD * PEERS), bf16),
            pltpu.VMEM((SPAN, WIDE), f32),
            pltpu.VMEM((RANK, BOX), bf16),
        ],
        compiler_params=pltpu.CompilerParams(vmem_limit_bytes=LIMIT),
        cost_estimate=pl.CostEstimate(flops=2 * 10**10, bytes_accessed=16 << 20, transcendentals=0),
        name="downward",
    )(far_op, near_a, near_b, served, own, source, m2l, m2m)


def on_device(child_poles, m2m_ops, m2l_ops, near_partner, near_op, far_source, far_target, far_op):
    child = child_poles.reshape(CHILD * RANK, BOX)
    source = far_source[0]
    poles, send = upward(child, m2m_ops, source, far_target[0])
    received = lax.all_to_all(send, ("curve", "sub"), split_axis=0, concat_axis=0, tiled=True)
    half = PAIRS // BATCH // 2
    near_a = near(near_op, poles, near_partner, m2l_ops, 0, half)
    answer = serve(poles, received)
    fetched = lax.all_to_all(answer, ("curve", "sub"), split_axis=0, concat_axis=0, tiled=True)
    near_b = near(near_op, poles, near_partner, m2l_ops, half * BATCH, PAIRS // BATCH - half)
    own = jnp.transpose(received, (2, 1, 0))
    served = jnp.transpose(fetched, (2, 1, 0))
    out = downward(far_op, near_a, near_b, served, own, source, m2l_ops, m2m_ops)
    return out.reshape(CHILD, RANK, BOX)


def solution(mesh):
    placed = (
        P(None, None, ("curve", "sub")),
        P(),
        P(),
        P(None, ("curve", "sub")),
        P(),
        P(("curve", "sub"), None, None),
        P(("curve", "sub"), None, None),
        P(),
    )
    return jax.shard_map(
        on_device,
        mesh=mesh,
        in_specs=placed,
        out_specs=P(None, None, ("curve", "sub")),
        check_vma=False,
    )
```

time: 2360 us -> 191 us (0.08); the launches traced: 2310 us -> 190 us
  other arithmetic: 1220 us -> 0 us
  local copies, waits for them, and re-layouts: 1000 us -> 20.1 us
  Pallas kernels: 0 us -> 148 us
  matrix products: 55 us -> 0 us
    scatter-add x13 -> x0, other arithmetic: 1190 us -> none  [the longest x11 987 us: near_step(): local = local.at[:, index.reshape(-1)].add(back.reshape(rank, -1))]
    gather x28 -> x0, local copies, waits for them, and re-layouts: 825 us -> none  [the longest x22 688 us: near_step(): fetched = jnp.take(poles, index, axis=1)]
    pallas_call x0 -> x5, Pallas kernels: none -> 148 us  [the longest x2 93.1 us: near(): pl.pallas_call(functools.partial(near_kernel, first, batches), out_shape=...]
    reshape x24 -> x0, local copies, waits for them, and re-layouts: 114 us -> none  [the longest x22 100 us: near_step(): local = local.at[:, index.reshape(-1)].add(back.reshape(rank, -1))]
    dot_general x25 -> x0, matrix products: 54.4 us -> none  [the longest x11 24.9 us: near_step(): jnp.einsum('jik,kjb->ib', operators, fetched, preferred_element_type=jnp....]
  transfers between devices with their start and end apart: 3 -> 2, of which waited for: 1 -> 0; matrix products, arithmetic and copies ran while one was open for 90% -> 7% of each run, Pallas kernels for 0% -> 49%
where the time goes in v1:
time: 191 us; the launch traced here: 190 us
  Pallas kernels  148 us (77%)
  starting transfers between devices  21.7 us (11%)
  local copies, waits for them, and re-layouts  20.1 us (11%)
    pallas_call x2, Pallas kernels, near(): pl.pallas_call(functools.partial(near_kernel, first, batches), out_shape=...  93.1 us
    pallas_call x1, Pallas kernels, downward(): pl.pallas_call(down_kernel, out_shape=jax.ShapeDtypeStruct((CHILD * RANK,...  27.5 us
    pallas_call x1, Pallas kernels, serve(): pl.pallas_call(serve_kernel, out_shape=jax.ShapeDtypeStruct((PEERS, RANK,...  13.9 us
    pallas_call x1, Pallas kernels, upward(): pl.pallas_call(up_kernel, out_shape=(jax.ShapeDtypeStruct((RANK, BOX), bf...  13.6 us
    unnamed x5, local copies, waits for them, and re-layouts  11.6 us
    all_to_all x1, starting transfers between devices, on_device(): lax.all_to_all(send, ('curve', 'sub'), split_axis=0, concat_axis=0, tiled...  11.5 us
    all_to_all x1, starting transfers between devices, on_device(): lax.all_to_all(answer, ('curve', 'sub'), split_axis=0, concat_axis=0, til...  10.2 us
    all_to_all x1, local copies, waits for them, and re-layouts, on_device(): lax.all_to_all(answer, ('curve', 'sub'), split_axis=0, concat_axis=0, til...  4.57 us
  transfers between devices with their start and end apart: 2, of which 0 were waited for; matrix products, arithmetic and copies ran while one was open for 7% of the time, Pallas kernels for 49%

profile of v1, /device:TPU:1, one launch (start us, length us, event | category | flops | bytes accessed | tf_op | source)
XLA Modules:
  0.0 190.0 jit_solution(11792293008954830887)
XLA Ops:
  0.0 13.6 %upward.1 = (bf16[64,2048]{1,0:T(8,128)(2,1)}, bf16[128,80,128]{2,1,0:T(8,128)(2,1)}) custom-call(bf16[512,2048]{1,0:T(8,128)(2,1)} %bitcast.8, bf16[8,64,64]{2,1,0:T(8,128)(2,1)} %m2m_ref.3, s32[128,128]{1,0:T(8,128)} %bitcast.10, s32[128,128]{1,0:T(8,128)} %bitcast.9), custom_call_target="tpu_custom_call" | custom-call | flops 10000000000 | bytes 6291456 | tf_op jit(solution)/shard_map/upward/pallas_call | solution.py:120
  13.6 11.5 %all-to-all-start = ((bf16[128,80,128]{2,1,0:T(8,128)(2,1)}), bf16[128,80,128]{2,1,0:T(8,128)(2,1)S(1)}, u32[]{:S(2)}, u32[]{:S(2)}) async-start(bf16[128,80,128]{2,1,0:T(8,128)(2,1)} %get-tuple-element.8), calls=%async_computation | async-start | bytes 5242880 | tf_op jit(solution)/shard_map/all_to_all | solution.py:311
  25.2 10.0 %copy.23.m2l_ref = bf16[316,64,64]{2,1,0:T(8,128)(2,1)} copy(bf16[316,64,64]{0,2,1:T(8,128)(2,1)} %param.10) | data formatting | bytes 5177344 | tf_op args[2]
  35.2 46.6 %near.3.near_b_ref = f32[64,2048]{1,0:T(8,128)} custom-call(s32[88]{0:T(128)} %op_ref.4, bf16[64,2048]{1,0:T(8,128)(2,1)} %get-tuple-element.7.poles_ref, s32[88,2048]{1,0:T(8,128)} %partner_ref.3, bf16[316,64,64]{2,1,0:T(8,128)(2,1)} %copy.23.m2l_ref), custom_call_target="tpu_custom_call" | custom-call | flops 44000002048 | bytes 6291456 | tf_op jit(solution)/shard_map/near/pallas_call | solution.py:224
  81.8 0.0 all-to-all-done.received_ref
  81.8 0.0 copy-start
  81.8 1.5 copy-done
  83.3 13.9 %serve.1 = bf16[128,64,128]{2,1,0:T(8,128)(2,1)} custom-call(bf16[64,2048]{1,0:T(8,128)(2,1)} %get-tuple-element.7.poles_ref, bf16[128,80,128]{2,1,0:T(8,128)(2,1)} %copy-done), custom_call_target="tpu_custom_call" | custom-call | flops 10000000000 | bytes 4194304 | tf_op jit(solution)/shard_map/serve/pallas_call | solution.py:159
  97.2 10.2 %all-to-all-start.1 = ((bf16[128,64,128]{2,1,0:T(8,128)(2,1)}), bf16[128,64,128]{2,1,0:T(8,128)(2,1)}, u32[]{:S(2)}, u32[]{:S(2)}) async-start(bf16[128,64,128]{2,1,0:T(8,128)(2,1)} %serve.1), calls=%async_computation.1 | async-start | bytes 4194304 | tf_op jit(solution)/shard_map/all_to_all | solution.py:315
  107.4 0.0 copy-start.1
  107.4 46.5 %near.2.near_a_ref = f32[64,2048]{1,0:T(8,128)} custom-call(s32[88]{0:T(128)} %op_ref.4, bf16[64,2048]{1,0:T(8,128)(2,1)} %get-tuple-element.7.poles_ref, s32[88,2048]{1,0:T(8,128)} %partner_ref.3, bf16[316,64,64]{2,1,0:T(8,128)(2,1)} %copy.23.m2l_ref), custom_call_target="tpu_custom_call" | custom-call | flops 44000002048 | bytes 6291456 | tf_op jit(solution)/shard_map/near/pallas_call | solution.py:224
  153.9 0.0 copy-done.1
  153.9 3.9 %copy.26 = bf16[128,80,128]{0,1,2:T(8,128)(2,1)} copy(bf16[128,80,128]{2,1,0:T(8,128)(2,1)S(1)} %copy-done.1) | data formatting | bytes 5242880 | tf_op jit(solution)/shard_map/all_to_all | solution.py:311
  157.9 0.0 all-to-all-done.1
  157.9 4.6 %copy.25 = bf16[128,64,128]{0,1,2:T(8,128)(2,1)} copy(bf16[128,64,128]{2,1,0:T(8,128)(2,1)} %all-to-all-done.1) | data formatting | bytes 4194304 | tf_op jit(solution)/shard_map/all_to_all | solution.py:315
  162.5 27.5 %downward.1 = bf16[512,2048]{1,0:T(8,128)(2,1)} custom-call(s32[128]{0:T(128)} %op_ref.5, f32[64,2048]{1,0:T(8,128)} %near.2.near_a_ref, f32[64,2048]{1,0:T(8,128)} %near.3.near_b_ref, bf16[128,64,128]{2,1,0:T(8,128)(2,1)} %bitcast.7, bf16[128,80,128]{2,1,0:T(8,128)(2,1)} %bitcast.6, s32[128,128]{1,0:T(8,128)} %bitcast.11, ...), custom_call_target="tpu_custom_call" | custom-call | flops 20000000000 | bytes 16777216 | tf_op jit(solution)/shard_map/downward/pallas_call | solution.py:287
Async XLA Ops:
  13.6 68.2 %all-to-all-start = ((bf16[128,80,128]{2,1,0:T(8,128)(2,1)}), bf16[128,80,128]{2,1,0:T(8,128)(2,1)S(1)}, u32[]{:S(2)}, u32[]{:S(2)}) async-start(bf16[128,80,128]{2,1,0:T(8,128)(2,1)} %get-tuple-element.8), calls=%async_computation | async-start | bytes 5242880 | tf_op jit(solution)/shard_map/all_to_all | solution.py:311
  81.8 1.5 copy-start
  97.2 60.7 %all-to-all-start.1 = ((bf16[128,64,128]{2,1,0:T(8,128)(2,1)}), bf16[128,64,128]{2,1,0:T(8,128)(2,1)}, u32[]{:S(2)}, u32[]{:S(2)}) async-start(bf16[128,64,128]{2,1,0:T(8,128)(2,1)} %serve.1), calls=%async_computation.1 | async-start | bytes 4194304 | tf_op jit(solution)/shard_map/all_to_all | solution.py:315
  107.4 46.5 %copy-start.1 = (bf16[128,80,128]{2,1,0:T(8,128)(2,1)S(1)}, bf16[128,80,128]{2,1,0:T(8,128)(2,1)}, u32[]{:S(2)}) copy-start(bf16[128,80,128]{2,1,0:T(8,128)(2,1)} %copy-done) | copy-start | bytes 7864324

commit v2 on v1

v2 whole, which is shorter than its diff:
```python
import functools

import jax
import jax.numpy as jnp
from jax import lax
from jax.experimental import pallas as pl
from jax.experimental.pallas import tpu as pltpu
from jax.sharding import PartitionSpec as P

RANK = 64
CHILD = 8
BOX = 2048
PEERS = 128
CAP = 128
PAIRS = 88
LANES = 128
TB = 256
NB = BOX // TB
STACK = NB * RANK
BATCH = 4
WIDE = BATCH * RANK
SIDES = 4
FAR = 8
EMPTY = 512
SENT = RANK + 16
f32 = jnp.float32
bf16 = jnp.bfloat16
VMEM = pl.BlockSpec(memory_space=pltpu.VMEM)
LIMIT = 56 * 2**20
NT = (((1,), (1,)), ((), ()))
TN = (((0,), (0,)), ((), ()))


def fill_table(table_ref):
    table_ref[...] = lax.broadcasted_iota(jnp.int32, table_ref.shape, 0).astype(f32).astype(bf16)


def split_index(index):
    group = index >> 8
    place = jnp.where(index >= 0, index - group * TB, EMPTY)
    return place.astype(f32), jnp.maximum(group, 0).astype(f32)


def one_hot(table_ref, place):
    n = place.shape[1]
    row = jnp.broadcast_to(place, (16, n)).astype(bf16)
    parts = []
    for r in range(TB // 16):
        here = table_ref[r * 16:(r + 1) * 16, :]
        here = jnp.concatenate([here] * (n // LANES), axis=1)
        parts.append(jnp.where(here == row, jnp.ones((), bf16), jnp.zeros((), bf16)))
    return jnp.concatenate(parts, axis=0)


def pick_group(stacked, group, low=0):
    out = stacked[0:RANK]
    for k in range(low + 1, NB):
        out = jnp.where(group == float(k), stacked[(k - low) * RANK:(k - low + 1) * RANK], out)
    return out


def spread_group(values, group, low=0):
    n = values.shape[1]
    row = jnp.broadcast_to(group, (16, n)).astype(bf16)
    parts = []
    for k in range(low, NB):
        mask = row == jnp.array(k, bf16)
        parts += [jnp.where(mask, values[r * 16:(r + 1) * 16], jnp.zeros((), bf16)) for r in range(RANK // 16)]
    return jnp.concatenate(parts, axis=0)


def stack_groups(poles_ref, stack_ref):
    for k in range(NB):
        stack_ref[k * RANK:(k + 1) * RANK, :] = poles_ref[:, k * TB:(k + 1) * TB]


def side_by_side(rows, i):
    return jnp.concatenate([rows[i:i + 1], rows[i + 1:i + 2]], axis=1)


def gather_rows(table_ref, stack_ref, place_ref, group_ref, hot_ref, store):
    def step(n, _):
        at = pl.multiple_of(n * FAR, FAR)
        places = place_ref[pl.ds(at, FAR), :]
        groups = group_ref[pl.ds(at, FAR), :]
        for i in range(0, FAR, 2):
            hot_ref[i // 2] = one_hot(table_ref, side_by_side(places, i))
            found = jnp.dot(stack_ref[...], hot_ref[i // 2], preferred_element_type=f32)
            found = pick_group(found, side_by_side(groups, i)).astype(bf16)
            store(at + i, found[:, :CAP])
            store(at + i + 1, found[:, CAP:])
        return 0

    lax.fori_loop(0, PEERS // FAR, step, 0)


GATHER_SCRATCH = [
    pltpu.VMEM((TB, LANES), bf16),
    pltpu.VMEM((STACK, TB), bf16),
    pltpu.VMEM((PEERS, CAP), f32),
    pltpu.VMEM((PEERS, CAP), f32),
    pltpu.VMEM((FAR // 2, TB, 2 * CAP), bf16),
]


def ops_kernel(far_op_ref, near_op_ref, m2l_ref, out_ref, wide_ref):
    count = m2l_ref.shape[1]
    slots = CAP + PAIRS
    names = jnp.concatenate([far_op_ref[...], near_op_ref[...]], axis=1)
    hot = (lax.broadcasted_iota(jnp.int32, (count, slots), 0) == names).astype(f32)
    hot = jnp.transpose(hot).astype(bf16)
    for r in range(0, RANK, 4):
        some = lax.dot_general(hot, m2l_ref[r * RANK:(r + 4) * RANK, :], NT, preferred_element_type=f32)
        for i in range(4):
            pair = some[:, (i // 2) * LANES:(i // 2 + 1) * LANES]
            if i % 2:
                pair = pltpu.roll(pair, RANK, 1)
            wide_ref[pl.ds(r + i, slots, stride=RANK), :] = pair

    def narrow(n, _):
        for i in range(8):
            s = n * 8 + i
            out_ref[s] = wide_ref[pl.ds(pl.multiple_of(s * RANK, RANK), RANK), :][:, :RANK].astype(bf16)
        return 0

    lax.fori_loop(0, slots // 8, narrow, 0)


def pick_ops(far_op, near_op, m2l):
    slots = CAP + PAIRS
    return pl.pallas_call(
        ops_kernel,
        out_shape=jax.ShapeDtypeStruct((slots, RANK, RANK), bf16),
        in_specs=[VMEM] * 3,
        out_specs=VMEM,
        scratch_shapes=[pltpu.VMEM((slots * RANK, LANES), f32)],
        compiler_params=pltpu.CompilerParams(vmem_limit_bytes=LIMIT),
        cost_estimate=pl.CostEstimate(flops=10**9, bytes_accessed=8 << 20, transcendentals=0),
        name="pick_ops",
    )(far_op.reshape(1, CAP), near_op.reshape(1, PAIRS), jnp.transpose(m2l, (1, 2, 0)).reshape(RANK * RANK, -1))


def up_kernel(child_ref, m2m_ref, source_ref, target_ref, poles_ref, send_ref,
              ask_place_ref, ask_group_ref, table_ref, stack_ref, place_ref, group_ref, hot_ref):
    fill_table(table_ref)
    ops = jnp.concatenate([m2m_ref[c] for c in range(CHILD)], axis=1)
    for s in range(0, BOX, 512):
        poles_ref[:, s:s + 512] = jnp.dot(
            ops, child_ref[:, s:s + 512], preferred_element_type=f32).astype(bf16)
    stack_groups(poles_ref, stack_ref)
    place_ref[...], group_ref[...] = split_index(source_ref[...])
    ask_place_ref[...], ask_group_ref[...] = split_index(target_ref[...])
    sub = lax.broadcasted_iota(jnp.int32, (16, CAP), 0)

    def store(q, block):
        send_ref[q, 0:RANK, :] = block
        ask = jnp.where(sub == 0, ask_place_ref[pl.ds(q, 1), :],
                        jnp.where(sub == 1, ask_group_ref[pl.ds(q, 1), :], 0.0))
        send_ref[q, RANK:SENT, :] = ask.astype(bf16)

    gather_rows(table_ref, stack_ref, place_ref, group_ref, hot_ref, store)


def upward(child, m2m, source, target):
    return pl.pallas_call(
        up_kernel,
        out_shape=(jax.ShapeDtypeStruct((RANK, BOX), bf16), jax.ShapeDtypeStruct((PEERS, SENT, CAP), bf16)),
        in_specs=[VMEM] * 4,
        out_specs=(VMEM, VMEM),
        scratch_shapes=[pltpu.VMEM((PEERS, CAP), f32), pltpu.VMEM((PEERS, CAP), f32)] + GATHER_SCRATCH,
        compiler_params=pltpu.CompilerParams(vmem_limit_bytes=LIMIT),
        cost_estimate=pl.CostEstimate(flops=10**10, bytes_accessed=6 << 20, transcendentals=0),
        name="upward",
    )(child, m2m, source, target)


def serve_kernel(poles_ref, received_ref, out_ref, table_ref, stack_ref, place_ref, group_ref, hot_ref):
    fill_table(table_ref)
    stack_groups(poles_ref, stack_ref)

    def unpack(n, _):
        for i in range(8):
            ask = received_ref[n * 8 + i, RANK:SENT, :].astype(f32)
            place_ref[pl.ds(n * 8 + i, 1), :] = ask[0:1]
            group_ref[pl.ds(n * 8 + i, 1), :] = ask[1:2]
        return 0

    lax.fori_loop(0, PEERS // 8, unpack, 0)

    def store(d, block):
        out_ref[d, :, :] = block

    gather_rows(table_ref, stack_ref, place_ref, group_ref, hot_ref, store)


def serve(poles, received):
    return pl.pallas_call(
        serve_kernel,
        out_shape=jax.ShapeDtypeStruct((PEERS, RANK, CAP), bf16),
        in_specs=[VMEM] * 2,
        out_specs=VMEM,
        scratch_shapes=GATHER_SCRATCH,
        compiler_params=pltpu.CompilerParams(vmem_limit_bytes=LIMIT),
        cost_estimate=pl.CostEstimate(flops=10**10, bytes_accessed=4 << 20, transcendentals=0),
        name="serve",
    )(poles, received)


def near_kernel(first, batches, poles_ref, partner_ref, ops_ref, out_ref,
                table_ref, stack_ref, place_ref, group_ref, hot_ref, spread_ref, sum_ref, both_ref):
    fill_table(table_ref)
    stack_groups(poles_ref, stack_ref)
    for b in range(NB):
        for j in range(BATCH):
            partner = partner_ref[first + j * batches:first + (j + 1) * batches, b * TB:(b + 1) * TB]
            lanes = slice((b * BATCH + j) * TB, (b * BATCH + j + 1) * TB)
            place_ref[:, lanes], group_ref[:, lanes] = split_index(partner)
    out_ref[...] = jnp.zeros(out_ref.shape, f32)

    def batch(n, _):
        ops = [ops_ref[CAP + first + j * batches + n] for j in range(BATCH)]
        ops = jnp.concatenate(ops + [jnp.transpose(op) for op in ops], axis=1)
        for b in range(NB):
            block = slice(b * TB, (b + 1) * TB)
            rows = (NB - b) * RANK
            for j in range(BATCH):
                lanes = slice((b * BATCH + j) * TB, (b * BATCH + j + 1) * TB)
                side = (b * BATCH + j) % SIDES
                place = place_ref[pl.ds(n, 1), lanes]
                group = group_ref[pl.ds(n, 1), lanes]
                hot_ref[side] = one_hot(table_ref, place)
                found = jnp.dot(stack_ref[b * RANK:, :], hot_ref[side], preferred_element_type=f32)
                both_ref[j * RANK:(j + 1) * RANK, block] = pick_group(found, group, b).astype(bf16)
                spread_ref[side, :rows, :] = spread_group(poles_ref[:, block], group, b)
                added = lax.dot_general(spread_ref[side, :rows, :], hot_ref[side], NT, preferred_element_type=f32)
                if b > 0:
                    added += sum_ref[j, b * RANK:, :]
                done = WIDE + j * RANK
                both_ref[done:done + RANK, block] = added[0:RANK].astype(bf16)
                if b < NB - 1:
                    sum_ref[j, (b + 1) * RANK:, :] = added[RANK:]
        out_ref[...] += jnp.dot(ops, both_ref[...], preferred_element_type=f32)
        return 0

    lax.fori_loop(0, batches, batch, 0)


def near(poles, partner, ops, first, batches):
    return pl.pallas_call(
        functools.partial(near_kernel, first, batches),
        out_shape=jax.ShapeDtypeStruct((RANK, BOX), f32),
        in_specs=[VMEM] * 3,
        out_specs=VMEM,
        scratch_shapes=[
            pltpu.VMEM((TB, LANES), bf16),
            pltpu.VMEM((STACK, TB), bf16),
            pltpu.VMEM((batches, BATCH * BOX), f32),
            pltpu.VMEM((batches, BATCH * BOX), f32),
            pltpu.VMEM((SIDES, TB, TB), bf16),
            pltpu.VMEM((SIDES, STACK, TB), bf16),
            pltpu.VMEM((BATCH, STACK, TB), f32),
            pltpu.VMEM((2 * WIDE, BOX), bf16),
        ],
        compiler_params=pltpu.CompilerParams(vmem_limit_bytes=LIMIT),
        cost_estimate=pl.CostEstimate(flops=10**9 * batches * BATCH, bytes_accessed=6 << 20, transcendentals=0),
        name="near",
    )(poles, partner, ops)


def down_kernel(near_a_ref, near_b_ref, served_ref, own_ref, source_ref, ops_ref, m2m_ref, out_ref,
                table_ref, place_ref, group_ref, hot_ref, spread_ref, total_ref, local_ref):
    fill_table(table_ref)
    place, group = split_index(source_ref[...])
    place_ref[...] = jnp.transpose(place)
    group_ref[...] = jnp.transpose(group)
    total_ref[...] = jnp.zeros(total_ref.shape, f32)

    def step(n, _):
        at = pl.multiple_of(n * FAR, FAR)
        source_places = place_ref[pl.ds(at, FAR), :]
        source_groups = group_ref[pl.ds(at, FAR), :]
        for i in range(0, FAR, 2):
            back, ahead, places, groups = [], [], [], []
            for k in range(2):
                c = at + i + k
                op = ops_ref[c]
                ahead.append(jnp.dot(op, served_ref[c], preferred_element_type=f32).astype(bf16))
                back.append(lax.dot_general(op, own_ref[c, 0:RANK, :], TN, preferred_element_type=f32).astype(bf16))
                ask = own_ref[c, RANK:SENT, :].astype(f32)
                places.append(ask[0:1])
                groups.append(ask[1:2])
            lanes = slice(2 * i * PEERS, (2 * i + 2) * PEERS)
            hot_ref[:, lanes] = one_hot(table_ref, side_by_side(source_places, i))
            spread_ref[:, lanes] = spread_group(jnp.concatenate(ahead, axis=1), side_by_side(source_groups, i))
            lanes = slice((2 * i + 2) * PEERS, (2 * i + 4) * PEERS)
            hot_ref[:, lanes] = one_hot(table_ref, jnp.concatenate(places, axis=1))
            spread_ref[:, lanes] = spread_group(jnp.concatenate(back, axis=1), jnp.concatenate(groups, axis=1))
        total_ref[...] += lax.dot_general(spread_ref[...], hot_ref[...], NT, preferred_element_type=f32)
        return 0

    lax.fori_loop(0, CAP // FAR, step, 0)
    ops = jnp.concatenate([m2m_ref[c] for c in range(CHILD)], axis=1)
    for k in range(NB):
        cols = slice(k * TB, (k + 1) * TB)
        far = total_ref[k * RANK:(k + 1) * RANK, :]
        local_ref[:, cols] = (near_a_ref[:, cols] + near_b_ref[:, cols] + far).astype(bf16)
        out_ref[:, cols] = lax.dot_general(
            ops, local_ref[:, cols], TN, preferred_element_type=f32).astype(bf16)


def downward(near_a, near_b, served, own, source, ops, m2m):
    return pl.pallas_call(
        down_kernel,
        out_shape=jax.ShapeDtypeStruct((CHILD * RANK, BOX), bf16),
        in_specs=[VMEM] * 7,
        out_specs=VMEM,
        scratch_shapes=[
            pltpu.VMEM((TB, LANES), bf16),
            pltpu.VMEM((CAP, PEERS), f32),
            pltpu.VMEM((CAP, PEERS), f32),
            pltpu.VMEM((TB, 2 * FAR * PEERS), bf16),
            pltpu.VMEM((STACK, 2 * FAR * PEERS), bf16),
            pltpu.VMEM((STACK, TB), f32),
            pltpu.VMEM((RANK, BOX), bf16),
        ],
        compiler_params=pltpu.CompilerParams(vmem_limit_bytes=LIMIT),
        cost_estimate=pl.CostEstimate(flops=2 * 10**10, bytes_accessed=16 << 20, transcendentals=0),
        name="downward",
    )(near_a, near_b, served, own, source, ops, m2m)


def on_device(child_poles, m2m_ops, m2l_ops, near_partner, near_op, far_source, far_target, far_op):
    child = child_poles.reshape(CHILD * RANK, BOX)
    source = far_source[0]
    poles, send = upward(child, m2m_ops, source, far_target[0])
    received = lax.all_to_all(send, ("curve", "sub"), split_axis=0, concat_axis=0, tiled=True)
    ops = pick_ops(far_op, near_op, m2l_ops)
    half = PAIRS // BATCH // 2
    near_a = near(poles, near_partner, ops, 0, half)
    answer = serve(poles, received)
    fetched = lax.all_to_all(answer, ("curve", "sub"), split_axis=0, concat_axis=0, tiled=True)
    near_b = near(poles, near_partner, ops, half * BATCH, PAIRS // BATCH - half)
    own = jnp.transpose(received, (2, 1, 0))
    served = jnp.transpose(fetched, (2, 1, 0))
    out = downward(near_a, near_b, served, own, source, ops, m2m_ops)
    return out.reshape(CHILD, RANK, BOX)


def solution(mesh):
    placed = (
        P(None, None, ("curve", "sub")),
        P(),
        P(),
        P(None, ("curve", "sub")),
        P(),
        P(("curve", "sub"), None, None),
        P(("curve", "sub"), None, None),
        P(),
    )
    return jax.shard_map(
        on_device,
        mesh=mesh,
        in_specs=placed,
        out_specs=P(None, None, ("curve", "sub")),
        check_vma=False,
    )
```

time: 191 us -> 162 us (0.85)
  Pallas kernels: 148 us -> 130 us
  local copies, waits for them, and re-layouts: 20.1 us -> 10 us
    pallas_call x2, Pallas kernels: 93.1 us -> 79.3 us  [near(): pl.pallas_call(functools.partial(near_kernel, first, batches), out_shape=...]
    unnamed x5 -> x4, local copies, waits for them, and re-layouts: 11.6 us -> 1.5 us
    pallas_call x0 -> x1, Pallas kernels: none -> 8.92 us  [pick_ops(): pl.pallas_call(ops_kernel, out_shape=jax.ShapeDtypeStruct((slots, RANK, R...]
    pallas_call x1, Pallas kernels: 27.5 us -> 20.1 us  [downward(): pl.pallas_call(down_kernel, out_shape=jax.ShapeDtypeStruct((CHILD * RANK,...]
    pallas_call x1, Pallas kernels: 13.9 us -> 10.4 us  [serve(): pl.pallas_call(serve_kernel, out_shape=jax.ShapeDtypeStruct((PEERS, RANK,...]
    pallas_call x1, Pallas kernels: 13.6 us -> 10.9 us  [upward(): pl.pallas_call(up_kernel, out_shape=(jax.ShapeDtypeStruct((RANK, BOX), bf...]
  transfers between devices with their start and end apart: 2 -> 2, of which waited for: 0 -> 0; matrix products, arithmetic and copies ran while one was open for 7% -> 2% of each run, Pallas kernels for 49% -> 55%
where the time goes in v2:
time: 162 us; the launch traced here: 161 us
  Pallas kernels  130 us (80%)
  starting transfers between devices  21.7 us (13%)
  local copies, waits for them, and re-layouts  10 us (6%)
    pallas_call x2, Pallas kernels, near(): pl.pallas_call(functools.partial(near_kernel, first, batches), out_shape=...  79.3 us
    pallas_call x1, Pallas kernels, downward(): pl.pallas_call(down_kernel, out_shape=jax.ShapeDtypeStruct((CHILD * RANK,...  20.1 us
    all_to_all x1, starting transfers between devices, on_device(): lax.all_to_all(send, ('curve', 'sub'), split_axis=0, concat_axis=0, tiled...  11.5 us
    pallas_call x1, Pallas kernels, upward(): pl.pallas_call(up_kernel, out_shape=(jax.ShapeDtypeStruct((RANK, BOX), bf...  10.9 us
    pallas_call x1, Pallas kernels, serve(): pl.pallas_call(serve_kernel, out_shape=jax.ShapeDtypeStruct((PEERS, RANK,...  10.4 us
    all_to_all x1, starting transfers between devices, on_device(): lax.all_to_all(answer, ('curve', 'sub'), split_axis=0, concat_axis=0, til...  10.2 us
    pallas_call x1, Pallas kernels, pick_ops(): pl.pallas_call(ops_kernel, out_shape=jax.ShapeDtypeStruct((slots, RANK, R...  8.92 us
    all_to_all x1, local copies, waits for them, and re-layouts, on_device(): lax.all_to_all(answer, ('curve', 'sub'), split_axis=0, concat_axis=0, til...  4.57 us
  transfers between devices with their start and end apart: 2, of which 0 were waited for; matrix products, arithmetic and copies ran while one was open for 2% of the time, Pallas kernels for 55%

profile of v2, /device:TPU:1, one launch (start us, length us, event | category | flops | bytes accessed | tf_op | source)
XLA Modules:
  0.0 161.4 jit_solution(4020860855687748791)
XLA Ops:
  0.0 10.9 %upward.1 = (bf16[64,2048]{1,0:T(8,128)(2,1)}, bf16[128,80,128]{2,1,0:T(8,128)(2,1)}) custom-call(bf16[512,2048]{1,0:T(8,128)(2,1)} %bitcast.16, bf16[8,64,64]{2,1,0:T(8,128)(2,1)} %m2m_ref.3, s32[128,128]{1,0:T(8,128)} %bitcast.18, s32[128,128]{1,0:T(8,128)} %bitcast.17), custom_call_target="tpu_custom_call" | custom-call | flops 10000000000 | bytes 6291456 | tf_op jit(solution)/shard_map/upward/pallas_call | solution.py:165
  10.9 11.5 %all-to-all-start = ((bf16[128,80,128]{2,1,0:T(8,128)(2,1)}), bf16[128,80,128]{2,1,0:T(8,128)(2,1)S(1)}, u32[]{:S(2)}, u32[]{:S(2)}) async-start(bf16[128,80,128]{2,1,0:T(8,128)(2,1)} %get-tuple-element.8), calls=%async_computation | async-start | bytes 5242880 | tf_op jit(solution)/shard_map/all_to_all | solution.py:336
  22.4 8.9 %pick_ops.1.ops_ref = bf16[216,64,64]{2,1,0:T(8,128)(2,1)} custom-call(s32[1,128]{1,0:T(1,128)} %bitcast.14, s32[1,88]{1,0:T(1,128)} %bitcast.15, bf16[4096,316]{1,0:T(8,128)(2,1)} %bitcast.11), custom_call_target="tpu_custom_call" | custom-call | flops 1000000000 | bytes 8388608 | tf_op jit(solution)/shard_map/pick_ops/pallas_call | solution.py:131
  31.3 39.6 %near.3.near_b_ref = f32[64,2048]{1,0:T(8,128)} custom-call(bf16[64,2048]{1,0:T(8,128)(2,1)} %get-tuple-element.7.poles_ref, s32[88,2048]{1,0:T(8,128)} %partner_ref.3, bf16[216,64,64]{2,1,0:T(8,128)(2,1)} %pick_ops.1.ops_ref), custom_call_target="tpu_custom_call" | custom-call | flops 44000002048 | bytes 6291456 | tf_op jit(solution)/shard_map/near/pallas_call | solution.py:249
  70.9 0.0 all-to-all-done.received_ref
  70.9 0.0 copy-start
  70.9 1.5 copy-done
  72.4 10.4 %serve.1 = bf16[128,64,128]{2,1,0:T(8,128)(2,1)} custom-call(bf16[64,2048]{1,0:T(8,128)(2,1)} %get-tuple-element.7.poles_ref, bf16[128,80,128]{2,1,0:T(8,128)(2,1)} %copy-done), custom_call_target="tpu_custom_call" | custom-call | flops 10000000000 | bytes 4194304 | tf_op jit(solution)/shard_map/serve/pallas_call | solution.py:197
  82.9 10.2 %all-to-all-start.1 = ((bf16[128,64,128]{2,1,0:T(8,128)(2,1)}), bf16[128,64,128]{2,1,0:T(8,128)(2,1)}, u32[]{:S(2)}, u32[]{:S(2)}) async-start(bf16[128,64,128]{2,1,0:T(8,128)(2,1)} %serve.1), calls=%async_computation.1 | async-start | bytes 4194304 | tf_op jit(solution)/shard_map/all_to_all | solution.py:341
  93.1 0.0 copy-start.1
  93.1 39.7 %near.2.near_a_ref = f32[64,2048]{1,0:T(8,128)} custom-call(bf16[64,2048]{1,0:T(8,128)(2,1)} %get-tuple-element.7.poles_ref, s32[88,2048]{1,0:T(8,128)} %partner_ref.3, bf16[216,64,64]{2,1,0:T(8,128)(2,1)} %pick_ops.1.ops_ref), custom_call_target="tpu_custom_call" | custom-call | flops 44000002048 | bytes 6291456 | tf_op jit(solution)/shard_map/near/pallas_call | solution.py:249
  132.8 0.0 copy-done.1
  132.8 3.9 %copy.18 = bf16[128,80,128]{0,1,2:T(8,128)(2,1)} copy(bf16[128,80,128]{2,1,0:T(8,128)(2,1)S(1)} %copy-done.1) | data formatting | bytes 5242880 | tf_op jit(solution)/shard_map/all_to_all | solution.py:336
  136.7 0.0 all-to-all-done.1
  136.7 4.6 %copy.17 = bf16[128,64,128]{0,1,2:T(8,128)(2,1)} copy(bf16[128,64,128]{2,1,0:T(8,128)(2,1)} %all-to-all-done.1) | data formatting | bytes 4194304 | tf_op jit(solution)/shard_map/all_to_all | solution.py:341
  141.3 20.1 %downward.1 = bf16[512,2048]{1,0:T(8,128)(2,1)} custom-call(f32[64,2048]{1,0:T(8,128)} %near.2.near_a_ref, f32[64,2048]{1,0:T(8,128)} %near.3.near_b_ref, bf16[128,64,128]{2,1,0:T(8,128)(2,1)} %bitcast.13, bf16[128,80,128]{2,1,0:T(8,128)(2,1)} %bitcast.12, s32[128,128]{1,0:T(8,128)} %bitcast.19, bf16[216,64,64]{2,1,0:T(8,128)(2,1)} %pick_ops.1.ops_ref, ...), custom_call_target="tpu_custom_call" | custom-call | flops 20000000000 | bytes 16777216 | tf_op jit(solution)/shard_map/downward/pallas_call | solution.py:312
Async XLA Ops:
  10.9 60.0 %all-to-all-start = ((bf16[128,80,128]{2,1,0:T(8,128)(2,1)}), bf16[128,80,128]{2,1,0:T(8,128)(2,1)S(1)}, u32[]{:S(2)}, u32[]{:S(2)}) async-start(bf16[128,80,128]{2,1,0:T(8,128)(2,1)} %get-tuple-element.8), calls=%async_computation | async-start | bytes 5242880 | tf_op jit(solution)/shard_map/all_to_all | solution.py:336
  70.9 1.5 copy-start
  82.9 53.9 %all-to-all-start.1 = ((bf16[128,64,128]{2,1,0:T(8,128)(2,1)}), bf16[128,64,128]{2,1,0:T(8,128)(2,1)}, u32[]{:S(2)}, u32[]{:S(2)}) async-start(bf16[128,64,128]{2,1,0:T(8,128)(2,1)} %serve.1), calls=%async_computation.1 | async-start | bytes 4194304 | tf_op jit(solution)/shard_map/all_to_all | solution.py:341
  93.1 39.7 %copy-start.1 = (bf16[128,80,128]{2,1,0:T(8,128)(2,1)S(1)}, bf16[128,80,128]{2,1,0:T(8,128)(2,1)}, u32[]{:S(2)}) copy-start(bf16[128,80,128]{2,1,0:T(8,128)(2,1)} %copy-done) | copy-start | bytes 7864324

commit v3 on v2

--- a/solution.py
+++ b/solution.py
@@ -17,9 +17,10 @@
 TB = 256
 NB = BOX // TB
 STACK = NB * RANK
-BATCH = 4
+BATCH = 8
 WIDE = BATCH * RANK
 SIDES = 4
+BY_LANE = 3
 FAR = 8
 EMPTY = 512
 SENT = RANK + 16
@@ -27,6 +28,7 @@
 bf16 = jnp.bfloat16
 VMEM = pl.BlockSpec(memory_space=pltpu.VMEM)
 LIMIT = 56 * 2**20
+ANY = pl.BlockSpec(memory_space=pl.ANY)
 NT = (((1,), (1,)), ((), ()))
 TN = (((0,), (0,)), ((), ()))
 
@@ -78,7 +80,7 @@
     return jnp.concatenate([rows[i:i + 1], rows[i + 1:i + 2]], axis=1)
 
 
-def gather_rows(table_ref, stack_ref, place_ref, group_ref, hot_ref, store):
+def gather_rows(table_ref, stack_ref, place_ref, group_ref, hot_ref, store, flush):
     def step(n, _):
         at = pl.multiple_of(n * FAR, FAR)
         places = place_ref[pl.ds(at, FAR), :]
@@ -89,6 +91,7 @@
             found = pick_group(found, side_by_side(groups, i)).astype(bf16)
             store(at + i, found[:, :CAP])
             store(at + i + 1, found[:, CAP:])
+        flush(at)
         return 0
 
     lax.fori_loop(0, PEERS // FAR, step, 0)
@@ -103,12 +106,13 @@
 ]
 
 
-def ops_kernel(far_op_ref, near_op_ref, m2l_ref, out_ref, wide_ref):
+def select_ops(far_op_ref, near_op_ref, m2l_ref, ready, far_ref, near_ref, wide_ref):
     count = m2l_ref.shape[1]
     slots = CAP + PAIRS
     names = jnp.concatenate([far_op_ref[...], near_op_ref[...]], axis=1)
     hot = (lax.broadcasted_iota(jnp.int32, (count, slots), 0) == names).astype(f32)
     hot = jnp.transpose(hot).astype(bf16)
+    ready()
     for r in range(0, RANK, 4):
         some = lax.dot_general(hot, m2l_ref[r * RANK:(r + 4) * RANK, :], NT, preferred_element_type=f32)
         for i in range(4):
@@ -116,38 +120,40 @@
             if i % 2:
                 pair = pltpu.roll(pair, RANK, 1)
             wide_ref[pl.ds(r + i, slots, stride=RANK), :] = pair
-
-    def narrow(n, _):
-        for i in range(8):
-            s = n * 8 + i
-            out_ref[s] = wide_ref[pl.ds(pl.multiple_of(s * RANK, RANK), RANK), :][:, :RANK].astype(bf16)
-        return 0
-
-    lax.fori_loop(0, slots // 8, narrow, 0)
-
-
-def pick_ops(far_op, near_op, m2l):
-    slots = CAP + PAIRS
-    return pl.pallas_call(
-        ops_kernel,
-        out_shape=jax.ShapeDtypeStruct((slots, RANK, RANK), bf16),
-        in_specs=[VMEM] * 3,
-        out_specs=VMEM,
-        scratch_shapes=[pltpu.VMEM((slots * RANK, LANES), f32)],
-        compiler_params=pltpu.CompilerParams(vmem_limit_bytes=LIMIT),
-        cost_estimate=pl.CostEstimate(flops=10**9, bytes_accessed=8 << 20, transcendentals=0),
-        name="pick_ops",
-    )(far_op.reshape(1, CAP), near_op.reshape(1, PAIRS), jnp.transpose(m2l, (1, 2, 0)).reshape(RANK * RANK, -1))
-
-
-def up_kernel(child_ref, m2m_ref, source_ref, target_ref, poles_ref, send_ref,
-              ask_place_ref, ask_group_ref, table_ref, stack_ref, place_ref, group_ref, hot_ref):
+    for out_ref, start in ((near_ref, CAP), (far_ref, 0)):
+        def narrow(n, _):
+            for i in range(8):
+                s = n * 8 + i
+                row = pl.multiple_of((start + s) * RANK, RANK)
+                out_ref[s] = wide_ref[pl.ds(row, RANK), :][:, :RANK].astype(bf16)
+            return 0
+
+        lax.fori_loop(0, out_ref.shape[0] // 8, narrow, 0)
+
+
+def up_kernel(child_any, source_any, target_any, m2l_any, m2m_ref, far_op_ref, near_op_ref,
+              poles_any, send_any, far_any, near_any,
+              child_ref, source_ref, target_ref, m2l_ref, poles_ref, send_ref, far_ref, near_ref, wide_ref,
+              in_sem, out_sem, ask_place_ref, ask_group_ref, table_ref, stack_ref, place_ref, group_ref, hot_ref):
+    part = BOX // 4
+    copies = [pltpu.make_async_copy(child_any.at[:, i * part:(i + 1) * part],
+                                    child_ref.at[:, i * part:(i + 1) * part], in_sem.at[i]) for i in range(4)]
+    copies += [pltpu.make_async_copy(source_any, source_ref, in_sem.at[4]),
+               pltpu.make_async_copy(target_any, target_ref, in_sem.at[5]),
+               pltpu.make_async_copy(m2l_any, m2l_ref, in_sem.at[6])]
+    for copy in copies:
+        copy.start()
     fill_table(table_ref)
     ops = jnp.concatenate([m2m_ref[c] for c in range(CHILD)], axis=1)
-    for s in range(0, BOX, 512):
-        poles_ref[:, s:s + 512] = jnp.dot(
-            ops, child_ref[:, s:s + 512], preferred_element_type=f32).astype(bf16)
+    for i in range(4):
+        cols = slice(i * part, (i + 1) * part)
+        copies[i].wait()
+        poles_ref[:, cols] = jnp.dot(ops, child_ref[:, cols], preferred_element_type=f32).astype(bf16)
+    poles_out = pltpu.make_async_copy(poles_ref, poles_any, out_sem.at[0])
+    poles_out.start()
     stack_groups(poles_ref, stack_ref)
+    copies[4].wait()
+    copies[5].wait()
     place_ref[...], group_ref[...] = split_index(source_ref[...])
     ask_place_ref[...], ask_group_ref[...] = split_index(target_ref[...])
     sub = lax.broadcasted_iota(jnp.int32, (16, CAP), 0)
@@ -158,29 +164,64 @@
                         jnp.where(sub == 1, ask_group_ref[pl.ds(q, 1), :], 0.0))
         send_ref[q, RANK:SENT, :] = ask.astype(bf16)
 
-    gather_rows(table_ref, stack_ref, place_ref, group_ref, hot_ref, store)
-
-
-def upward(child, m2m, source, target):
+    def flush(q):
+        pltpu.make_async_copy(send_ref.at[pl.ds(q, FAR)], send_any.at[pl.ds(q, FAR)], out_sem.at[1]).start()
+
+    gather_rows(table_ref, stack_ref, place_ref, group_ref, hot_ref, store, flush)
+    select_ops(far_op_ref, near_op_ref, m2l_ref, copies[6].wait, far_ref, near_ref, wide_ref)
+    near_out = pltpu.make_async_copy(near_ref, near_any, out_sem.at[2])
+    far_out = pltpu.make_async_copy(far_ref, far_any, out_sem.at[3])
+    near_out.start()
+    far_out.start()
+    poles_out.wait()
+    pltpu.make_async_copy(send_ref, send_any, out_sem.at[1]).wait()
+    near_out.wait()
+    far_out.wait()
+
+
+def upward(child, m2m, source, target, far_op, near_op, m2l):
+    slots = CAP + PAIRS
+    flat = jnp.transpose(m2l, (1, 2, 0)).reshape(RANK * RANK, -1)
+    out_shape = (
+        jax.ShapeDtypeStruct((RANK, BOX), bf16),
+        jax.ShapeDtypeStruct((PEERS, SENT, CAP), bf16),
+        jax.ShapeDtypeStruct((CAP, RANK, RANK), bf16),
+        jax.ShapeDtypeStruct((PAIRS, RANK, RANK), bf16),
+    )
     return pl.pallas_call(
         up_kernel,
-        out_shape=(jax.ShapeDtypeStruct((RANK, BOX), bf16), jax.ShapeDtypeStruct((PEERS, SENT, CAP), bf16)),
-        in_specs=[VMEM] * 4,
-        out_specs=(VMEM, VMEM),
-        scratch_shapes=[pltpu.VMEM((PEERS, CAP), f32), pltpu.VMEM((PEERS, CAP), f32)] + GATHER_SCRATCH,
+        out_shape=out_shape,
+        in_specs=[ANY] * 4 + [VMEM] * 3,
+        out_specs=(ANY,) * 4,
+        scratch_shapes=[
+            pltpu.VMEM(child.shape, bf16),
+            pltpu.VMEM(source.shape, jnp.int32),
+            pltpu.VMEM(target.shape, jnp.int32),
+            pltpu.VMEM(flat.shape, bf16),
+        ] + [pltpu.VMEM(o.shape, o.dtype) for o in out_shape] + [
+            pltpu.VMEM((slots * RANK, LANES), f32),
+            pltpu.SemaphoreType.DMA((7,)),
+            pltpu.SemaphoreType.DMA((4,)),
+            pltpu.VMEM((PEERS, CAP), f32),
+            pltpu.VMEM((PEERS, CAP), f32),
+        ] + GATHER_SCRATCH,
         compiler_params=pltpu.CompilerParams(vmem_limit_bytes=LIMIT),
-        cost_estimate=pl.CostEstimate(flops=10**10, bytes_accessed=6 << 20, transcendentals=0),
+        cost_estimate=pl.CostEstimate(flops=10**10, bytes_accessed=12 << 20, transcendentals=0),
         name="upward",
-    )(child, m2m, source, target)
-
-
-def serve_kernel(poles_ref, received_ref, out_ref, table_ref, stack_ref, place_ref, group_ref, hot_ref):
+    )(child, source, target, flat, m2m, far_op.reshape(1, CAP), near_op.reshape(1, PAIRS))
+
+
+def serve_kernel(poles_ref, received_any, out_any, out_ref, ask_ref, in_sem, out_sem,
+                 table_ref, stack_ref, place_ref, group_ref, hot_ref):
+    asked = pltpu.make_async_copy(received_any.at[:, RANK:SENT, :], ask_ref, in_sem)
+    asked.start()
     fill_table(table_ref)
     stack_groups(poles_ref, stack_ref)
+    asked.wait()
 
     def unpack(n, _):
         for i in range(8):
-            ask = received_ref[n * 8 + i, RANK:SENT, :].astype(f32)
+            ask = ask_ref[n * 8 + i].astype(f32)
             place_ref[pl.ds(n * 8 + i, 1), :] = ask[0:1]
             group_ref[pl.ds(n * 8 + i, 1), :] = ask[1:2]
         return 0
@@ -190,35 +231,65 @@
     def store(d, block):
         out_ref[d, :, :] = block
 
-    gather_rows(table_ref, stack_ref, place_ref, group_ref, hot_ref, store)
+    def flush(d):
+        pltpu.make_async_copy(out_ref.at[pl.ds(d, FAR)], out_any.at[pl.ds(d, FAR)], out_sem).start()
+
+    gather_rows(table_ref, stack_ref, place_ref, group_ref, hot_ref, store, flush)
+    pltpu.make_async_copy(out_ref, out_any, out_sem).wait()
 
 
 def serve(poles, received):
     return pl.pallas_call(
         serve_kernel,
         out_shape=jax.ShapeDtypeStruct((PEERS, RANK, CAP), bf16),
-        in_specs=[VMEM] * 2,
-        out_specs=VMEM,
-        scratch_shapes=GATHER_SCRATCH,
+        in_specs=[VMEM, ANY],
+        out_specs=ANY,
+        scratch_shapes=[
+            pltpu.VMEM((PEERS, RANK, CAP), bf16),
+            pltpu.VMEM((PEERS, SENT - RANK, CAP), bf16),
+            pltpu.SemaphoreType.DMA,
+            pltpu.SemaphoreType.DMA,
+        ] + GATHER_SCRATCH,
         compiler_params=pltpu.CompilerParams(vmem_limit_bytes=LIMIT),
         cost_estimate=pl.CostEstimate(flops=10**10, bytes_accessed=4 << 20, transcendentals=0),
         name="serve",
     )(poles, received)
 
 
+def pick_lanes(poles_ref, lane, chunk, b):
+    columns = []
+    for t in range(TB // LANES):
+        first = b * (TB // LANES) + t
+        at = jnp.broadcast_to(lane[:, t * LANES:(t + 1) * LANES], (8, LANES)).astype(jnp.int32)
+        where = jnp.broadcast_to(chunk[:, t * LANES:(t + 1) * LANES], (8, LANES))
+        found = [jnp.zeros((8, LANES), f32)] * (RANK // 8)
+        for k in range(first, BOX // LANES):
+            mask = where == float(k)
+            for r in range(RANK // 8):
+                moved = jnp.take_along_axis(poles_ref[r * 8:(r + 1) * 8, k * LANES:(k + 1) * LANES], at, axis=1)
+                found[r] = jnp.where(mask, moved, found[r])
+        columns.append(jnp.concatenate(found, axis=0))
+    return jnp.concatenate(columns, axis=1)
+
+
 def near_kernel(first, batches, poles_ref, partner_ref, ops_ref, out_ref,
-                table_ref, stack_ref, place_ref, group_ref, hot_ref, spread_ref, sum_ref, both_ref):
+                table_ref, stack_ref, place_ref, group_ref, lane_ref, chunk_ref, poles32_ref, hot_ref, spread_ref,
+                sum_ref, both_ref):
     fill_table(table_ref)
+    poles32_ref[...] = poles_ref[...].astype(f32)
     stack_groups(poles_ref, stack_ref)
     for b in range(NB):
         for j in range(BATCH):
             partner = partner_ref[first + j * batches:first + (j + 1) * batches, b * TB:(b + 1) * TB]
             lanes = slice((b * BATCH + j) * TB, (b * BATCH + j + 1) * TB)
             place_ref[:, lanes], group_ref[:, lanes] = split_index(partner)
+            if b >= BY_LANE:
+                lane_ref[:, lanes] = (partner & (LANES - 1)).astype(f32)
+                chunk_ref[:, lanes] = (partner >> 7).astype(f32)
     out_ref[...] = jnp.zeros(out_ref.shape, f32)
 
     def batch(n, _):
-        ops = [ops_ref[CAP + first + j * batches + n] for j in range(BATCH)]
+        ops = [ops_ref[first + j * batches + n] for j in range(BATCH)]
         ops = jnp.concatenate(ops + [jnp.transpose(op) for op in ops], axis=1)
         for b in range(NB):
             block = slice(b * TB, (b + 1) * TB)
@@ -229,8 +300,14 @@
                 place = place_ref[pl.ds(n, 1), lanes]
                 group = group_ref[pl.ds(n, 1), lanes]
                 hot_ref[side] = one_hot(table_ref, place)
-                found = jnp.dot(stack_ref[b * RANK:, :], hot_ref[side], preferred_element_type=f32)
-                both_ref[j * RANK:(j + 1) * RANK, block] = pick_group(found, group, b).astype(bf16)
+                if b < BY_LANE:
+                    found = jnp.dot(stack_ref[b * RANK:, :], hot_ref[side], preferred_element_type=f32)
+                    both_ref[j * RANK:(j + 1) * RANK, block] = pick_group(found, group, b).astype(bf16)
+                o = NB - 1 - b
+                if o >= BY_LANE:
+                    lanes = slice((o * BATCH + j) * TB, (o * BATCH + j + 1) * TB)
+                    picked = pick_lanes(poles32_ref, lane_ref[pl.ds(n, 1), lanes], chunk_ref[pl.ds(n, 1), lanes], o)
+                    both_ref[j * RANK:(j + 1) * RANK, o * TB:(o + 1) * TB] = picked.astype(bf16)
                 spread_ref[side, :rows, :] = spread_group(poles_ref[:, block], group, b)
                 added = lax.dot_general(spread_ref[side, :rows, :], hot_ref[side], NT, preferred_element_type=f32)
                 if b > 0:
@@ -256,6 +333,9 @@
             pltpu.VMEM((STACK, TB), bf16),
             pltpu.VMEM((batches, BATCH * BOX), f32),
             pltpu.VMEM((batches, BATCH * BOX), f32),
+            pltpu.VMEM((batches, BATCH * BOX), f32),
+            pltpu.VMEM((batches, BATCH * BOX), f32),
+            pltpu.VMEM((RANK, BOX), f32),
             pltpu.VMEM((SIDES, TB, TB), bf16),
             pltpu.VMEM((SIDES, STACK, TB), bf16),
             pltpu.VMEM((BATCH, STACK, TB), f32),
@@ -267,8 +347,17 @@
     )(poles, partner, ops)
 
 
-def down_kernel(near_a_ref, near_b_ref, served_ref, own_ref, source_ref, ops_ref, m2m_ref, out_ref,
+def down_kernel(served_any, own_any, near_a_ref, near_b_ref, source_ref, ops_ref, m2m_ref, out_any,
+                served_ref, own_ref, out_ref, in_sem, out_sem,
                 table_ref, place_ref, group_ref, hot_ref, spread_ref, total_ref, local_ref):
+    def fetch(n):
+        rows = pl.ds(n * FAR, FAR)
+        return (pltpu.make_async_copy(served_any.at[rows], served_ref.at[rows], in_sem.at[0, n]),
+                pltpu.make_async_copy(own_any.at[rows], own_ref.at[rows], in_sem.at[1, n]))
+
+    for n in range(CAP // FAR):
+        for copy in fetch(n):
+            copy.start()
     fill_table(table_ref)
     place, group = split_index(source_ref[...])
     place_ref[...] = jnp.transpose(place)
@@ -277,8 +366,11 @@
 
     def step(n, _):
         at = pl.multiple_of(n * FAR, FAR)
+        for copy in fetch(n):
+            copy.wait()
         source_places = place_ref[pl.ds(at, FAR), :]
         source_groups = group_ref[pl.ds(at, FAR), :]
+
         for i in range(0, FAR, 2):
             back, ahead, places, groups = [], [], [], []
             for k in range(2):
@@ -306,15 +398,24 @@
         local_ref[:, cols] = (near_a_ref[:, cols] + near_b_ref[:, cols] + far).astype(bf16)
         out_ref[:, cols] = lax.dot_general(
             ops, local_ref[:, cols], TN, preferred_element_type=f32).astype(bf16)
+        if k % 4 == 3:
+            cols = slice((k - 3) * TB, (k + 1) * TB)
+            pltpu.make_async_copy(out_ref.at[:, cols], out_any.at[:, cols], out_sem).start()
+    pltpu.make_async_copy(out_ref, out_any, out_sem).wait()
 
 
 def downward(near_a, near_b, served, own, source, ops, m2m):
     return pl.pallas_call(
         down_kernel,
         out_shape=jax.ShapeDtypeStruct((CHILD * RANK, BOX), bf16),
-        in_specs=[VMEM] * 7,
-        out_specs=VMEM,
+        in_specs=[ANY] * 2 + [VMEM] * 5,
+        out_specs=ANY,
         scratch_shapes=[
+            pltpu.VMEM(served.shape, bf16),
+            pltpu.VMEM(own.shape, bf16),
+            pltpu.VMEM((CHILD * RANK, BOX), bf16),
+            pltpu.SemaphoreType.DMA((2, CAP // FAR)),
+            pltpu.SemaphoreType.DMA,
             pltpu.VMEM((TB, LANES), bf16),
             pltpu.VMEM((CAP, PEERS), f32),
             pltpu.VMEM((CAP, PEERS), f32),
@@ -326,23 +427,22 @@
         compiler_params=pltpu.CompilerParams(vmem_limit_bytes=LIMIT),
         cost_estimate=pl.CostEstimate(flops=2 * 10**10, bytes_accessed=16 << 20, transcendentals=0),
         name="downward",
-    )(near_a, near_b, served, own, source, ops, m2m)
+    )(served, own, near_a, near_b, source, ops, m2m)
 
 
 def on_device(child_poles, m2m_ops, m2l_ops, near_partner, near_op, far_source, far_target, far_op):
     child = child_poles.reshape(CHILD * RANK, BOX)
     source = far_source[0]
-    poles, send = upward(child, m2m_ops, source, far_target[0])
+    poles, send, far_ops, near_ops = upward(child, m2m_ops, source, far_target[0], far_op, near_op, m2l_ops)
     received = lax.all_to_all(send, ("curve", "sub"), split_axis=0, concat_axis=0, tiled=True)
-    ops = pick_ops(far_op, near_op, m2l_ops)
-    half = PAIRS // BATCH // 2
-    near_a = near(poles, near_partner, ops, 0, half)
+    half = (PAIRS // BATCH + 1) // 2
+    near_a = near(poles, near_partner, near_ops, 0, half)
     answer = serve(poles, received)
     fetched = lax.all_to_all(answer, ("curve", "sub"), split_axis=0, concat_axis=0, tiled=True)
-    near_b = near(poles, near_partner, ops, half * BATCH, PAIRS // BATCH - half)
+    near_b = near(poles, near_partner, near_ops, half * BATCH, PAIRS // BATCH - half)
     own = jnp.transpose(received, (2, 1, 0))
     served = jnp.transpose(fetched, (2, 1, 0))
-    out = downward(near_a, near_b, served, own, source, ops, m2m_ops)
+    out = downward(near_a, near_b, served, own, source, far_ops, m2m_ops)
     return out.reshape(CHILD, RANK, BOX)
 
 

time: 162 us -> 148 us (0.914)
  Pallas kernels: 130 us -> 115 us
    pallas_call x2, Pallas kernels: 79.3 us -> 69.1 us  [near(): pl.pallas_call(functools.partial(near_kernel, first, batches), out_shape=...]
    pallas_call x2 -> x1, Pallas kernels: 19.8 us -> 17.2 us  [upward(): pl.pallas_call(up_kernel, out_shape=out_shape, in_specs=[ANY] * 4 + [VMEM...]
  transfers between devices with their start and end apart: 2 -> 2, of which waited for: 0 -> 0; matrix products, arithmetic and copies ran while one was open for 2% -> 3% of each run, Pallas kernels for 55% -> 47%
where the time goes in v3:
time: 148 us; the launch traced here: 147 us
  Pallas kernels  115 us (78%)
  starting transfers between devices  21.7 us (15%)
  local copies, waits for them, and re-layouts  10 us (7%)
    pallas_call x2, Pallas kernels, near(): pl.pallas_call(functools.partial(near_kernel, first, batches), out_shape=...  69.1 us
    pallas_call x1, Pallas kernels, downward(): pl.pallas_call(down_kernel, out_shape=jax.ShapeDtypeStruct((CHILD * RANK,...  19.1 us
    pallas_call x1, Pallas kernels, upward(): pl.pallas_call(up_kernel, out_shape=out_shape, in_specs=[ANY] * 4 + [VMEM...  17.2 us
    all_to_all x1, starting transfers between devices, on_device(): lax.all_to_all(send, ('curve', 'sub'), split_axis=0, concat_axis=0, tiled...  11.5 us
    all_to_all x1, starting transfers between devices, on_device(): lax.all_to_all(answer, ('curve', 'sub'), split_axis=0, concat_axis=0, til...  10.2 us
    pallas_call x1, Pallas kernels, serve(): pl.pallas_call(serve_kernel, out_shape=jax.ShapeDtypeStruct((PEERS, RANK,...  9.91 us
    all_to_all x1, local copies, waits for them, and re-layouts, on_device(): lax.all_to_all(answer, ('curve', 'sub'), split_axis=0, concat_axis=0, til...  4.57 us
    all_to_all x1, local copies, waits for them, and re-layouts, on_device(): lax.all_to_all(send, ('curve', 'sub'), split_axis=0, concat_axis=0, tiled...  3.9 us
  transfers between devices with their start and end apart: 2, of which 0 were waited for; matrix products, arithmetic and copies ran while one was open for 3% of the time, Pallas kernels for 47%

profile of v3, /device:TPU:1, one launch (start us, length us, event | category | flops | bytes accessed | tf_op | source)
XLA Modules:
  0.0 147.3 jit_solution(1550844912103521583)
XLA Ops:
  0.0 17.2 %upward.1 = (bf16[64,2048]{1,0:T(8,128)(2,1)}, bf16[128,80,128]{2,1,0:T(8,128)(2,1)}, bf16[128,64,64]{2,1,0:T(8,128)(2,1)}, bf16[88,64,64]{2,1,0:T(8,128)(2,1)}) custom-call(bf16[512,2048]{1,0:T(8,128)(2,1)} %bitcast.14, s32[128,128]{1,0:T(8,128)} %bitcast.16, s32[128,128]{1,0:T(8,128)} %bitcast.15, bf16[4096,316]{1,0:T(8,128)(2,1)} %bitcast.13, ...), custom_call_target="tpu_custom_call" | custom-call | flops 10000000000 | bytes 12582912 | tf_op jit(solution)/shard_map/upward/pallas_call | solution.py:191
  17.2 11.5 %all-to-all-start = ((bf16[128,80,128]{2,1,0:T(8,128)(2,1)}), bf16[128,80,128]{2,1,0:T(8,128)(2,1)S(1)}, u32[]{:S(2)}, u32[]{:S(2)}) async-start(bf16[128,80,128]{2,1,0:T(8,128)(2,1)} %get-tuple-element.10), calls=%async_computation | async-start | bytes 5242880 | tf_op jit(solution)/shard_map/all_to_all | solution.py:437
  28.7 37.3 %near.2.near_a_ref = f32[64,2048]{1,0:T(8,128)} custom-call(bf16[64,2048]{1,0:T(8,128)(2,1)} %get-tuple-element.9.poles_ref, s32[88,2048]{1,0:T(8,128)} %partner_ref.3, bf16[88,64,64]{2,1,0:T(8,128)(2,1)} %get-tuple-element.11.ops_ref), custom_call_target="tpu_custom_call" | custom-call | flops 48000000000 | bytes 6291456 | tf_op jit(solution)/shard_map/near/pallas_call | solution.py:326
  66.1 0.0 all-to-all-done.received_any
  66.1 0.0 copy-start
  66.1 1.5 %copy-done = bf16[128,80,128]{2,1,0:T(8,128)(2,1)} copy-done((bf16[128,80,128]{2,1,0:T(8,128)(2,1)}, bf16[128,80,128]{2,1,0:T(8,128)(2,1)S(1)}, u32[]{:S(2)}) %copy-start) | copy-done | bytes 2621464
  67.6 9.9 %serve.1 = bf16[128,64,128]{2,1,0:T(8,128)(2,1)} custom-call(bf16[64,2048]{1,0:T(8,128)(2,1)} %get-tuple-element.9.poles_ref, bf16[128,80,128]{2,1,0:T(8,128)(2,1)} %copy-done), custom_call_target="tpu_custom_call" | custom-call | flops 10000000000 | bytes 4194304 | tf_op jit(solution)/shard_map/serve/pallas_call | solution.py:242
  77.5 10.2 %all-to-all-start.1 = ((bf16[128,64,128]{2,1,0:T(8,128)(2,1)}), bf16[128,64,128]{2,1,0:T(8,128)(2,1)}, u32[]{:S(2)}, u32[]{:S(2)}) async-start(bf16[128,64,128]{2,1,0:T(8,128)(2,1)} %serve.1), calls=%async_computation.1 | async-start | bytes 4194304 | tf_op jit(solution)/shard_map/all_to_all | solution.py:441
  87.8 0.0 copy-start.1
  87.8 31.7 %near.3.near_b_ref = f32[64,2048]{1,0:T(8,128)} custom-call(bf16[64,2048]{1,0:T(8,128)(2,1)} %get-tuple-element.9.poles_ref, s32[88,2048]{1,0:T(8,128)} %partner_ref.3, bf16[88,64,64]{2,1,0:T(8,128)(2,1)} %get-tuple-element.11.ops_ref), custom_call_target="tpu_custom_call" | custom-call | flops 40000000000 | bytes 6291456 | tf_op jit(solution)/shard_map/near/pallas_call | solution.py:326
  119.5 0.0 copy-done.1
  119.5 3.9 %copy.18 = bf16[128,80,128]{0,1,2:T(8,128)(2,1)} copy(bf16[128,80,128]{2,1,0:T(8,128)(2,1)S(1)} %copy-done.1) | data formatting | bytes 5242880 | tf_op jit(solution)/shard_map/all_to_all | solution.py:437
  123.4 0.0 all-to-all-done.1
  123.4 4.6 %copy.17 = bf16[128,64,128]{0,1,2:T(8,128)(2,1)} copy(bf16[128,64,128]{2,1,0:T(8,128)(2,1)} %all-to-all-done.1) | data formatting | bytes 4194304 | tf_op jit(solution)/shard_map/all_to_all | solution.py:441
  128.0 19.1 %downward.1 = bf16[512,2048]{1,0:T(8,128)(2,1)} custom-call(bf16[128,64,128]{2,1,0:T(8,128)(2,1)} %bitcast.12, bf16[128,80,128]{2,1,0:T(8,128)(2,1)} %bitcast.11, f32[64,2048]{1,0:T(8,128)} %near.2.near_a_ref, f32[64,2048]{1,0:T(8,128)} %near.3.near_b_ref, s32[128,128]{1,0:T(8,128)} %bitcast.17, bf16[128,64,64]{2,1,0:T(8,128)(2,1)} %get-tuple-element.12.ops_ref, ...), custom_call_target="tpu_custom_call" | custom-call | flops 20000000000 | bytes 16777216 | tf_op jit(solution)/shard_map/downward/pallas_call | solution.py:408
Async XLA Ops:
  17.2 48.9 %all-to-all-start = ((bf16[128,80,128]{2,1,0:T(8,128)(2,1)}), bf16[128,80,128]{2,1,0:T(8,128)(2,1)S(1)}, u32[]{:S(2)}, u32[]{:S(2)}) async-start(bf16[128,80,128]{2,1,0:T(8,128)(2,1)} %get-tuple-element.10), calls=%async_computation | async-start | bytes 5242880 | tf_op jit(solution)/shard_map/all_to_all | solution.py:437
  66.1 1.5 %copy-start = (bf16[128,80,128]{2,1,0:T(8,128)(2,1)}, bf16[128,80,128]{2,1,0:T(8,128)(2,1)S(1)}, u32[]{:S(2)}) copy-start(bf16[128,80,128]{2,1,0:T(8,128)(2,1)S(1)} %all-to-all-done.received_any) | copy-start | bytes 7864324
  77.5 45.9 %all-to-all-start.1 = ((bf16[128,64,128]{2,1,0:T(8,128)(2,1)}), bf16[128,64,128]{2,1,0:T(8,128)(2,1)}, u32[]{:S(2)}, u32[]{:S(2)}) async-start(bf16[128,64,128]{2,1,0:T(8,128)(2,1)} %serve.1), calls=%async_computation.1 | async-start | bytes 4194304 | tf_op jit(solution)/shard_map/all_to_all | solution.py:441
  87.8 31.7 %copy-start.1 = (bf16[128,80,128]{2,1,0:T(8,128)(2,1)S(1)}, bf16[128,80,128]{2,1,0:T(8,128)(2,1)}, u32[]{:S(2)}) copy-start(bf16[128,80,128]{2,1,0:T(8,128)(2,1)} %copy-done) | copy-start | bytes 7864324

commit v4 on v3

--- a/solution.py
+++ b/solution.py
@@ -106,34 +106,29 @@
 ]
 
 
-def select_ops(far_op_ref, near_op_ref, m2l_ref, ready, far_ref, near_ref, wide_ref):
+def select_ops(far_op_ref, near_op_ref, m2l_ref, ready, far_ref, near_ref):
     count = m2l_ref.shape[1]
-    slots = CAP + PAIRS
     names = jnp.concatenate([far_op_ref[...], near_op_ref[...]], axis=1)
-    hot = (lax.broadcasted_iota(jnp.int32, (count, slots), 0) == names).astype(f32)
+    hot = (lax.broadcasted_iota(jnp.int32, (count, CAP + PAIRS), 0) == names).astype(f32)
     hot = jnp.transpose(hot).astype(bf16)
     ready()
-    for r in range(0, RANK, 4):
-        some = lax.dot_general(hot, m2l_ref[r * RANK:(r + 4) * RANK, :], NT, preferred_element_type=f32)
-        for i in range(4):
-            pair = some[:, (i // 2) * LANES:(i // 2 + 1) * LANES]
-            if i % 2:
-                pair = pltpu.roll(pair, RANK, 1)
-            wide_ref[pl.ds(r + i, slots, stride=RANK), :] = pair
-    for out_ref, start in ((near_ref, CAP), (far_ref, 0)):
-        def narrow(n, _):
-            for i in range(8):
-                s = n * 8 + i
-                row = pl.multiple_of((start + s) * RANK, RANK)
-                out_ref[s] = wide_ref[pl.ds(row, RANK), :][:, :RANK].astype(bf16)
-            return 0
-
-        lax.fori_loop(0, out_ref.shape[0] // 8, narrow, 0)
+    for m in range(0, RANK // 2, 2):
+        rows = [m2l_ref[r * RANK:(r + 1) * RANK, :] for r in (m, m + RANK // 2, m + 1, m + 1 + RANK // 2)]
+        some = lax.dot_general(hot, jnp.concatenate(rows, axis=0), NT, preferred_element_type=f32)
+        for i in range(2):
+            pair = some[:, i * LANES:(i + 1) * LANES]
+            far_ref[(m + i) * CAP:(m + i + 1) * CAP, :] = pair[:CAP]
+            near_ref[(m + i) * PAIRS:(m + i + 1) * PAIRS, :] = pair[CAP:]
+
+
+def take_op(ops_ref, s, slots):
+    pairs = ops_ref[pl.ds(s, RANK // 2, stride=slots), :]
+    return jnp.concatenate([pairs[:, :RANK], pairs[:, RANK:]], axis=0).astype(bf16)
 
 
 def up_kernel(child_any, source_any, target_any, m2l_any, m2m_ref, far_op_ref, near_op_ref,
               poles_any, send_any, far_any, near_any,
-              child_ref, source_ref, target_ref, m2l_ref, poles_ref, send_ref, far_ref, near_ref, wide_ref,
+              child_ref, source_ref, target_ref, m2l_ref, poles_ref, send_ref, far_ref, near_ref,
               in_sem, out_sem, ask_place_ref, ask_group_ref, table_ref, stack_ref, place_ref, group_ref, hot_ref):
     part = BOX // 4
     copies = [pltpu.make_async_copy(child_any.at[:, i * part:(i + 1) * part],
@@ -168,7 +163,7 @@
         pltpu.make_async_copy(send_ref.at[pl.ds(q, FAR)], send_any.at[pl.ds(q, FAR)], out_sem.at[1]).start()
 
     gather_rows(table_ref, stack_ref, place_ref, group_ref, hot_ref, store, flush)
-    select_ops(far_op_ref, near_op_ref, m2l_ref, copies[6].wait, far_ref, near_ref, wide_ref)
+    select_ops(far_op_ref, near_op_ref, m2l_ref, copies[6].wait, far_ref, near_ref)
     near_out = pltpu.make_async_copy(near_ref, near_any, out_sem.at[2])
     far_out = pltpu.make_async_copy(far_ref, far_any, out_sem.at[3])
     near_out.start()
@@ -180,13 +175,12 @@
 
 
 def upward(child, m2m, source, target, far_op, near_op, m2l):
-    slots = CAP + PAIRS
     flat = jnp.transpose(m2l, (1, 2, 0)).reshape(RANK * RANK, -1)
     out_shape = (
         jax.ShapeDtypeStruct((RANK, BOX), bf16),
         jax.ShapeDtypeStruct((PEERS, SENT, CAP), bf16),
-        jax.ShapeDtypeStruct((CAP, RANK, RANK), bf16),
-        jax.ShapeDtypeStruct((PAIRS, RANK, RANK), bf16),
+        jax.ShapeDtypeStruct((RANK // 2 * CAP, LANES), f32),
+        jax.ShapeDtypeStruct((RANK // 2 * PAIRS, LANES), f32),
     )
     return pl.pallas_call(
         up_kernel,
@@ -199,7 +193,6 @@
             pltpu.VMEM(target.shape, jnp.int32),
             pltpu.VMEM(flat.shape, bf16),
         ] + [pltpu.VMEM(o.shape, o.dtype) for o in out_shape] + [
-            pltpu.VMEM((slots * RANK, LANES), f32),
             pltpu.SemaphoreType.DMA((7,)),
             pltpu.SemaphoreType.DMA((4,)),
             pltpu.VMEM((PEERS, CAP), f32),
@@ -289,7 +282,7 @@
     out_ref[...] = jnp.zeros(out_ref.shape, f32)
 
     def batch(n, _):
-        ops = [ops_ref[first + j * batches + n] for j in range(BATCH)]
+        ops = [take_op(ops_ref, first + j * batches + n, PAIRS) for j in range(BATCH)]
         ops = jnp.concatenate(ops + [jnp.transpose(op) for op in ops], axis=1)
         for b in range(NB):
             block = slice(b * TB, (b + 1) * TB)
@@ -375,7 +368,7 @@
             back, ahead, places, groups = [], [], [], []
             for k in range(2):
                 c = at + i + k
-                op = ops_ref[c]
+                op = take_op(ops_ref, c, CAP)
                 ahead.append(jnp.dot(op, served_ref[c], preferred_element_type=f32).astype(bf16))
                 back.append(lax.dot_general(op, own_ref[c, 0:RANK, :], TN, preferred_element_type=f32).astype(bf16))
                 ask = own_ref[c, RANK:SENT, :].astype(f32)

time: 148 us -> 145 us (0.980)
  Pallas kernels: 115 us -> 113 us
    pallas_call x1, Pallas kernels: 17.2 us -> 13.3 us  [upward(): pl.pallas_call(up_kernel, out_shape=out_shape, in_specs=[ANY] * 4 + [VMEM...]
  transfers between devices with their start and end apart: 2 -> 2, of which waited for: 0 -> 0; matrix products, arithmetic and copies ran while one was open for 3% -> 3% of each run, Pallas kernels for 47% -> 48%
where the time goes in v4:
time: 145 us
  Pallas kernels  113 us (78%)
  starting transfers between devices  21.7 us (15%)
  local copies, waits for them, and re-layouts  10 us (7%)
    pallas_call x2, Pallas kernels, near(): pl.pallas_call(functools.partial(near_kernel, first, batches), out_shape=...  69.2 us
    pallas_call x1, Pallas kernels, downward(): pl.pallas_call(down_kernel, out_shape=jax.ShapeDtypeStruct((CHILD * RANK,...  20.5 us
    pallas_call x1, Pallas kernels, upward(): pl.pallas_call(up_kernel, out_shape=out_shape, in_specs=[ANY] * 4 + [VMEM...  13.3 us
    all_to_all x1, starting transfers between devices, on_device(): lax.all_to_all(send, ('curve', 'sub'), split_axis=0, concat_axis=0, tiled...  11.5 us
    all_to_all x1, starting transfers between devices, on_device(): lax.all_to_all(answer, ('curve', 'sub'), split_axis=0, concat_axis=0, til...  10.2 us
    pallas_call x1, Pallas kernels, serve(): pl.pallas_call(serve_kernel, out_shape=jax.ShapeDtypeStruct((PEERS, RANK,...  9.91 us
    all_to_all x1, local copies, waits for them, and re-layouts, on_device(): lax.all_to_all(answer, ('curve', 'sub'), split_axis=0, concat_axis=0, til...  4.57 us
    all_to_all x1, local copies, waits for them, and re-layouts, on_device(): lax.all_to_all(send, ('curve', 'sub'), split_axis=0, concat_axis=0, tiled...  3.9 us
  transfers between devices with their start and end apart: 2, of which 0 were waited for; matrix products, arithmetic and copies ran while one was open for 3% of the time, Pallas kernels for 48%

profile of v4, /device:TPU:1, one launch (start us, length us, event | category | flops | bytes accessed | tf_op | source)
XLA Modules:
  0.0 144.9 jit_solution(365533472587037705)
XLA Ops:
  0.0 13.3 %upward.1 = (bf16[64,2048]{1,0:T(8,128)(2,1)}, bf16[128,80,128]{2,1,0:T(8,128)(2,1)}, f32[4096,128]{1,0:T(8,128)}, f32[2816,128]{1,0:T(8,128)}) custom-call(bf16[512,2048]{1,0:T(8,128)(2,1)} %bitcast.14, s32[128,128]{1,0:T(8,128)} %bitcast.16, s32[128,128]{1,0:T(8,128)} %bitcast.15, bf16[4096,316]{1,0:T(8,128)(2,1)} %bitcast.13, bf16[8,64,64]{2,1,0:T(8,128)(2,1)} %m2m_ref.3, ...), custom_call_target="tpu_custom_call" | custom-call | flops 10000000000 | bytes 12582912 | tf_op jit(solution)/shard_map/upward/pallas_call | solution.py:185
  13.4 11.5 %all-to-all-start = ((bf16[128,80,128]{2,1,0:T(8,128)(2,1)}), bf16[128,80,128]{2,1,0:T(8,128)(2,1)S(1)}, u32[]{:S(2)}, u32[]{:S(2)}) async-start(bf16[128,80,128]{2,1,0:T(8,128)(2,1)} %get-tuple-element.10), calls=%async_computation | async-start | bytes 5242880 | tf_op jit(solution)/shard_map/all_to_all | solution.py:430
  24.9 37.4 %near.2.near_a_ref = f32[64,2048]{1,0:T(8,128)} custom-call(bf16[64,2048]{1,0:T(8,128)(2,1)} %get-tuple-element.9.poles_ref, s32[88,2048]{1,0:T(8,128)} %partner_ref.3, f32[2816,128]{1,0:T(8,128)} %get-tuple-element.11.ops_ref), custom_call_target="tpu_custom_call" | custom-call | flops 48000000000 | bytes 6291456 | tf_op jit(solution)/shard_map/near/pallas_call | solution.py:319
  62.3 0.0 all-to-all-done.received_any
  62.3 0.0 copy-start
  62.3 1.5 %copy-done = bf16[128,80,128]{2,1,0:T(8,128)(2,1)} copy-done((bf16[128,80,128]{2,1,0:T(8,128)(2,1)}, bf16[128,80,128]{2,1,0:T(8,128)(2,1)S(1)}, u32[]{:S(2)}) %copy-start) | copy-done | bytes 2621464
  63.8 9.9 %serve.1 = bf16[128,64,128]{2,1,0:T(8,128)(2,1)} custom-call(bf16[64,2048]{1,0:T(8,128)(2,1)} %get-tuple-element.9.poles_ref, bf16[128,80,128]{2,1,0:T(8,128)(2,1)} %copy-done), custom_call_target="tpu_custom_call" | custom-call | flops 10000000000 | bytes 4194304 | tf_op jit(solution)/shard_map/serve/pallas_call | solution.py:235
  73.8 10.2 %all-to-all-start.1 = ((bf16[128,64,128]{2,1,0:T(8,128)(2,1)}), bf16[128,64,128]{2,1,0:T(8,128)(2,1)}, u32[]{:S(2)}, u32[]{:S(2)}) async-start(bf16[128,64,128]{2,1,0:T(8,128)(2,1)} %serve.1), calls=%async_computation.1 | async-start | bytes 4194304 | tf_op jit(solution)/shard_map/all_to_all | solution.py:434
  84.0 0.0 copy-start.1
  84.0 31.8 %near.3.near_b_ref = f32[64,2048]{1,0:T(8,128)} custom-call(bf16[64,2048]{1,0:T(8,128)(2,1)} %get-tuple-element.9.poles_ref, s32[88,2048]{1,0:T(8,128)} %partner_ref.3, f32[2816,128]{1,0:T(8,128)} %get-tuple-element.11.ops_ref), custom_call_target="tpu_custom_call" | custom-call | flops 40000000000 | bytes 6291456 | tf_op jit(solution)/shard_map/near/pallas_call | solution.py:319
  115.8 0.0 copy-done.1
  115.8 3.9 %copy.18 = bf16[128,80,128]{0,1,2:T(8,128)(2,1)} copy(bf16[128,80,128]{2,1,0:T(8,128)(2,1)S(1)} %copy-done.1) | data formatting | bytes 5242880 | tf_op jit(solution)/shard_map/all_to_all | solution.py:430
  119.7 0.0 all-to-all-done.1
  119.7 4.6 %copy.17 = bf16[128,64,128]{0,1,2:T(8,128)(2,1)} copy(bf16[128,64,128]{2,1,0:T(8,128)(2,1)} %all-to-all-done.1) | data formatting | bytes 4194304 | tf_op jit(solution)/shard_map/all_to_all | solution.py:434
  124.3 20.5 %downward.1 = bf16[512,2048]{1,0:T(8,128)(2,1)} custom-call(bf16[128,64,128]{2,1,0:T(8,128)(2,1)} %bitcast.12, bf16[128,80,128]{2,1,0:T(8,128)(2,1)} %bitcast.11, f32[64,2048]{1,0:T(8,128)} %near.2.near_a_ref, f32[64,2048]{1,0:T(8,128)} %near.3.near_b_ref, s32[128,128]{1,0:T(8,128)} %bitcast.17, f32[4096,128]{1,0:T(8,128)} %get-tuple-element.12.ops_ref, ...), custom_call_target="tpu_custom_call" | custom-call | flops 20000000000 | bytes 16777216 | tf_op jit(solution)/shard_map/downward/pallas_call | solution.py:401
Async XLA Ops:
  13.4 49.0 %all-to-all-start = ((bf16[128,80,128]{2,1,0:T(8,128)(2,1)}), bf16[128,80,128]{2,1,0:T(8,128)(2,1)S(1)}, u32[]{:S(2)}, u32[]{:S(2)}) async-start(bf16[128,80,128]{2,1,0:T(8,128)(2,1)} %get-tuple-element.10), calls=%async_computation | async-start | bytes 5242880 | tf_op jit(solution)/shard_map/all_to_all | solution.py:430
  62.3 1.5 %copy-start = (bf16[128,80,128]{2,1,0:T(8,128)(2,1)}, bf16[128,80,128]{2,1,0:T(8,128)(2,1)S(1)}, u32[]{:S(2)}) copy-start(bf16[128,80,128]{2,1,0:T(8,128)(2,1)S(1)} %all-to-all-done.received_any) | copy-start | bytes 7864324
  73.8 45.9 %all-to-all-start.1 = ((bf16[128,64,128]{2,1,0:T(8,128)(2,1)}), bf16[128,64,128]{2,1,0:T(8,128)(2,1)}, u32[]{:S(2)}, u32[]{:S(2)}) async-start(bf16[128,64,128]{2,1,0:T(8,128)(2,1)} %serve.1), calls=%async_computation.1 | async-start | bytes 4194304 | tf_op jit(solution)/shard_map/all_to_all | solution.py:434
  84.0 31.8 %copy-start.1 = (bf16[128,80,128]{2,1,0:T(8,128)(2,1)S(1)}, bf16[128,80,128]{2,1,0:T(8,128)(2,1)}, u32[]{:S(2)}) copy-start(bf16[128,80,128]{2,1,0:T(8,128)(2,1)} %copy-done) | copy-start | bytes 7864324

commit v5 on v4

--- a/solution.py
+++ b/solution.py
@@ -20,7 +20,7 @@
 BATCH = 8
 WIDE = BATCH * RANK
 SIDES = 4
-BY_LANE = 3
+BY_LANE = 2
 FAR = 8
 EMPTY = 512
 SENT = RANK + 16
@@ -162,12 +162,12 @@
     def flush(q):
         pltpu.make_async_copy(send_ref.at[pl.ds(q, FAR)], send_any.at[pl.ds(q, FAR)], out_sem.at[1]).start()
 
-    gather_rows(table_ref, stack_ref, place_ref, group_ref, hot_ref, store, flush)
     select_ops(far_op_ref, near_op_ref, m2l_ref, copies[6].wait, far_ref, near_ref)
     near_out = pltpu.make_async_copy(near_ref, near_any, out_sem.at[2])
     far_out = pltpu.make_async_copy(far_ref, far_any, out_sem.at[3])
     near_out.start()
     far_out.start()
+    gather_rows(table_ref, stack_ref, place_ref, group_ref, hot_ref, store, flush)
     poles_out.wait()
     pltpu.make_async_copy(send_ref, send_any, out_sem.at[1]).wait()
     near_out.wait()
@@ -204,12 +204,17 @@
     )(child, source, target, flat, m2m, far_op.reshape(1, CAP), near_op.reshape(1, PAIRS))
 
 
-def serve_kernel(poles_ref, received_any, out_any, out_ref, ask_ref, in_sem, out_sem,
+def serve_kernel(poles_any, received_any, out_any, out_ref, ask_ref, in_sem, pole_sem, out_sem,
                  table_ref, stack_ref, place_ref, group_ref, hot_ref):
     asked = pltpu.make_async_copy(received_any.at[:, RANK:SENT, :], ask_ref, in_sem)
     asked.start()
+    poles = [pltpu.make_async_copy(poles_any.at[:, k * TB:(k + 1) * TB],
+                                   stack_ref.at[k * RANK:(k + 1) * RANK, :], pole_sem.at[k]) for k in range(NB)]
+    for copy in poles:
+        copy.start()
     fill_table(table_ref)
-    stack_groups(poles_ref, stack_ref)
+    for copy in poles:
+        copy.wait()
     asked.wait()
 
     def unpack(n, _):
@@ -235,12 +240,13 @@
     return pl.pallas_call(
         serve_kernel,
         out_shape=jax.ShapeDtypeStruct((PEERS, RANK, CAP), bf16),
-        in_specs=[VMEM, ANY],
+        in_specs=[ANY, ANY],
         out_specs=ANY,
         scratch_shapes=[
             pltpu.VMEM((PEERS, RANK, CAP), bf16),
             pltpu.VMEM((PEERS, SENT - RANK, CAP), bf16),
             pltpu.SemaphoreType.DMA,
+            pltpu.SemaphoreType.DMA((NB,)),
             pltpu.SemaphoreType.DMA,
         ] + GATHER_SCRATCH,
         compiler_params=pltpu.CompilerParams(vmem_limit_bytes=LIMIT),
@@ -340,17 +346,23 @@
     )(poles, partner, ops)
 
 
-def down_kernel(served_any, own_any, near_a_ref, near_b_ref, source_ref, ops_ref, m2m_ref, out_any,
-                served_ref, own_ref, out_ref, in_sem, out_sem,
+def down_kernel(served_any, own_any, ops_any, near_a_any, near_b_any, source_ref, m2m_ref, out_any,
+                served_ref, own_ref, ops_ref, near_a_ref, near_b_ref, out_ref, in_sem, more_sem, out_sem,
                 table_ref, place_ref, group_ref, hot_ref, spread_ref, total_ref, local_ref):
     def fetch(n):
         rows = pl.ds(n * FAR, FAR)
         return (pltpu.make_async_copy(served_any.at[rows], served_ref.at[rows], in_sem.at[0, n]),
                 pltpu.make_async_copy(own_any.at[rows], own_ref.at[rows], in_sem.at[1, n]))
 
-    for n in range(CAP // FAR):
+    more = [pltpu.make_async_copy(a, b, more_sem.at[i]) for i, (a, b) in enumerate(
+        ((ops_any, ops_ref), (near_a_any, near_a_ref), (near_b_any, near_b_ref)))]
+    for copy in fetch(0) + tuple(more[:1]):
+        copy.start()
+    for n in range(1, CAP // FAR):
         for copy in fetch(n):
             copy.start()
+    for copy in more[1:]:
+        copy.start()
     fill_table(table_ref)
     place, group = split_index(source_ref[...])
     place_ref[...] = jnp.transpose(place)
@@ -383,7 +395,10 @@
         total_ref[...] += lax.dot_general(spread_ref[...], hot_ref[...], NT, preferred_element_type=f32)
         return 0
 
+    more[0].wait()
     lax.fori_loop(0, CAP // FAR, step, 0)
+    more[1].wait()
+    more[2].wait()
     ops = jnp.concatenate([m2m_ref[c] for c in range(CHILD)], axis=1)
     for k in range(NB):
         cols = slice(k * TB, (k + 1) * TB)
@@ -401,13 +416,17 @@
     return pl.pallas_call(
         down_kernel,
         out_shape=jax.ShapeDtypeStruct((CHILD * RANK, BOX), bf16),
-        in_specs=[ANY] * 2 + [VMEM] * 5,
+        in_specs=[ANY] * 5 + [VMEM] * 2,
         out_specs=ANY,
         scratch_shapes=[
             pltpu.VMEM(served.shape, bf16),
             pltpu.VMEM(own.shape, bf16),
+            pltpu.VMEM(ops.shape, f32),
+            pltpu.VMEM((RANK, BOX), f32),
+            pltpu.VMEM((RANK, BOX), f32),
             pltpu.VMEM((CHILD * RANK, BOX), bf16),
             pltpu.SemaphoreType.DMA((2, CAP // FAR)),
+            pltpu.SemaphoreType.DMA((3,)),
             pltpu.SemaphoreType.DMA,
             pltpu.VMEM((TB, LANES), bf16),
             pltpu.VMEM((CAP, PEERS), f32),
@@ -420,7 +439,7 @@
         compiler_params=pltpu.CompilerParams(vmem_limit_bytes=LIMIT),
         cost_estimate=pl.CostEstimate(flops=2 * 10**10, bytes_accessed=16 << 20, transcendentals=0),
         name="downward",
-    )(served, own, near_a, near_b, source, ops, m2m)
+    )(served, own, ops, near_a, near_b, source, m2m)
 
 
 def on_device(child_poles, m2m_ops, m2l_ops, near_partner, near_op, far_source, far_target, far_op):

time: 145 us -> 145 us (level)
  no operation moved by 1% of the time
where the time goes in v5:
time: 145 us; the launch traced here: 144 us
  Pallas kernels  112 us (77%)
  starting transfers between devices  21.7 us (15%)
  local copies, waits for them, and re-layouts  10 us (7%)
    pallas_call x2, Pallas kernels, near(): pl.pallas_call(functools.partial(near_kernel, first, batches), out_shape=...  68.7 us
    pallas_call x1, Pallas kernels, downward(): pl.pallas_call(down_kernel, out_shape=jax.ShapeDtypeStruct((CHILD * RANK,...  21.7 us
    pallas_call x1, Pallas kernels, upward(): pl.pallas_call(up_kernel, out_shape=out_shape, in_specs=[ANY] * 4 + [VMEM...  12.7 us
    all_to_all x1, starting transfers between devices, on_device(): lax.all_to_all(send, ('curve', 'sub'), split_axis=0, concat_axis=0, tiled...  11.5 us
    all_to_all x1, starting transfers between devices, on_device(): lax.all_to_all(answer, ('curve', 'sub'), split_axis=0, concat_axis=0, til...  10.2 us
    pallas_call x1, Pallas kernels, serve(): pl.pallas_call(serve_kernel, out_shape=jax.ShapeDtypeStruct((PEERS, RANK,...  9.17 us
    all_to_all x1, local copies, waits for them, and re-layouts, on_device(): lax.all_to_all(answer, ('curve', 'sub'), split_axis=0, concat_axis=0, til...  4.57 us
    all_to_all x1, local copies, waits for them, and re-layouts, on_device(): lax.all_to_all(send, ('curve', 'sub'), split_axis=0, concat_axis=0, tiled...  3.9 us
  transfers between devices with their start and end apart: 2, of which 0 were waited for; matrix products, arithmetic and copies ran while one was open for 3% of the time, Pallas kernels for 48%

profile of v5, /device:TPU:1, one launch (start us, length us, event | category | flops | bytes accessed | tf_op | source)
XLA Modules:
  0.0 144.3 jit_solution(12950039965958165474)
XLA Ops:
  0.0 12.7 %upward.1 = (bf16[64,2048]{1,0:T(8,128)(2,1)}, bf16[128,80,128]{2,1,0:T(8,128)(2,1)}, f32[4096,128]{1,0:T(8,128)}, f32[2816,128]{1,0:T(8,128)}) custom-call(bf16[512,2048]{1,0:T(8,128)(2,1)} %bitcast.14, s32[128,128]{1,0:T(8,128)} %bitcast.16, s32[128,128]{1,0:T(8,128)} %bitcast.15, bf16[4096,316]{1,0:T(8,128)(2,1)} %bitcast.13, bf16[8,64,64]{2,1,0:T(8,128)(2,1)} %m2m_ref.3, ...), custom_call_target="tpu_custom_call" | custom-call | flops 10000000000 | bytes 12582912 | tf_op jit(solution)/shard_map/upward/pallas_call | solution.py:185
  12.7 11.5 %all-to-all-start = ((bf16[128,80,128]{2,1,0:T(8,128)(2,1)}), bf16[128,80,128]{2,1,0:T(8,128)(2,1)S(1)}, u32[]{:S(2)}, u32[]{:S(2)}) async-start(bf16[128,80,128]{2,1,0:T(8,128)(2,1)} %get-tuple-element.10), calls=%async_computation | async-start | bytes 5242880 | tf_op jit(solution)/shard_map/all_to_all | solution.py:449
  24.3 37.2 %near.2.near_a_any = f32[64,2048]{1,0:T(8,128)} custom-call(bf16[64,2048]{1,0:T(8,128)(2,1)} %get-tuple-element.9.poles_any.poles_ref, s32[88,2048]{1,0:T(8,128)} %partner_ref.3, f32[2816,128]{1,0:T(8,128)} %get-tuple-element.12.ops_ref), custom_call_target="tpu_custom_call" | custom-call | flops 48000000000 | bytes 6291456 | tf_op jit(solution)/shard_map/near/pallas_call | solution.py:325
  61.4 0.0 all-to-all-done.received_any
  61.4 0.0 copy-start
  61.4 1.5 %copy-done = bf16[128,80,128]{2,1,0:T(8,128)(2,1)} copy-done((bf16[128,80,128]{2,1,0:T(8,128)(2,1)}, bf16[128,80,128]{2,1,0:T(8,128)(2,1)S(1)}, u32[]{:S(2)}) %copy-start) | copy-done | bytes 2621464
  62.9 9.2 %serve.1 = bf16[128,64,128]{2,1,0:T(8,128)(2,1)} custom-call(bf16[64,2048]{1,0:T(8,128)(2,1)} %get-tuple-element.9.poles_any.poles_ref, bf16[128,80,128]{2,1,0:T(8,128)(2,1)} %copy-done), custom_call_target="tpu_custom_call" | custom-call | flops 10000000000 | bytes 4194304 | tf_op jit(solution)/shard_map/serve/pallas_call | solution.py:240
  72.1 10.2 %all-to-all-start.1 = ((bf16[128,64,128]{2,1,0:T(8,128)(2,1)}), bf16[128,64,128]{2,1,0:T(8,128)(2,1)}, u32[]{:S(2)}, u32[]{:S(2)}) async-start(bf16[128,64,128]{2,1,0:T(8,128)(2,1)} %serve.1), calls=%async_computation.1 | async-start | bytes 4194304 | tf_op jit(solution)/shard_map/all_to_all | solution.py:453
  82.4 0.0 copy-start.1
  82.4 31.6 %near.3.near_b_any = f32[64,2048]{1,0:T(8,128)} custom-call(bf16[64,2048]{1,0:T(8,128)(2,1)} %get-tuple-element.9.poles_any.poles_ref, s32[88,2048]{1,0:T(8,128)} %partner_ref.3, f32[2816,128]{1,0:T(8,128)} %get-tuple-element.12.ops_ref), custom_call_target="tpu_custom_call" | custom-call | flops 40000000000 | bytes 6291456 | tf_op jit(solution)/shard_map/near/pallas_call | solution.py:325
  113.9 0.0 copy-done.1
  113.9 3.9 %copy.18 = bf16[128,80,128]{0,1,2:T(8,128)(2,1)} copy(bf16[128,80,128]{2,1,0:T(8,128)(2,1)S(1)} %copy-done.1) | data formatting | bytes 5242880 | tf_op jit(solution)/shard_map/all_to_all | solution.py:449
  117.9 0.0 all-to-all-done.1
  117.9 4.6 %copy.17 = bf16[128,64,128]{0,1,2:T(8,128)(2,1)} copy(bf16[128,64,128]{2,1,0:T(8,128)(2,1)} %all-to-all-done.1) | data formatting | bytes 4194304 | tf_op jit(solution)/shard_map/all_to_all | solution.py:453
  122.4 21.7 %downward.1 = bf16[512,2048]{1,0:T(8,128)(2,1)} custom-call(bf16[128,64,128]{2,1,0:T(8,128)(2,1)} %bitcast.12, bf16[128,80,128]{2,1,0:T(8,128)(2,1)} %bitcast.11, f32[4096,128]{1,0:T(8,128)} %get-tuple-element.11.ops_any, f32[64,2048]{1,0:T(8,128)} %near.2.near_a_any, f32[64,2048]{1,0:T(8,128)} %near.3.near_b_any, s32[128,128]{1,0:T(8,128)} %bitcast.17, ...), custom_call_target="tpu_custom_call" | custom-call | flops 20000000000 | bytes 16777216 | tf_op jit(solution)/shard_map/downward/pallas_call | solution.py:416
Async XLA Ops:
  12.7 48.7 %all-to-all-start = ((bf16[128,80,128]{2,1,0:T(8,128)(2,1)}), bf16[128,80,128]{2,1,0:T(8,128)(2,1)S(1)}, u32[]{:S(2)}, u32[]{:S(2)}) async-start(bf16[128,80,128]{2,1,0:T(8,128)(2,1)} %get-tuple-element.10), calls=%async_computation | async-start | bytes 5242880 | tf_op jit(solution)/shard_map/all_to_all | solution.py:449
  61.4 1.5 %copy-start = (bf16[128,80,128]{2,1,0:T(8,128)(2,1)}, bf16[128,80,128]{2,1,0:T(8,128)(2,1)S(1)}, u32[]{:S(2)}) copy-start(bf16[128,80,128]{2,1,0:T(8,128)(2,1)S(1)} %all-to-all-done.received_any) | copy-start | bytes 7864324
  72.1 45.7 %all-to-all-start.1 = ((bf16[128,64,128]{2,1,0:T(8,128)(2,1)}), bf16[128,64,128]{2,1,0:T(8,128)(2,1)}, u32[]{:S(2)}, u32[]{:S(2)}) async-start(bf16[128,64,128]{2,1,0:T(8,128)(2,1)} %serve.1), calls=%async_computation.1 | async-start | bytes 4194304 | tf_op jit(solution)/shard_map/all_to_all | solution.py:453
  82.4 31.6 %copy-start.1 = (bf16[128,80,128]{2,1,0:T(8,128)(2,1)S(1)}, bf16[128,80,128]{2,1,0:T(8,128)(2,1)}, u32[]{:S(2)}) copy-start(bf16[128,80,128]{2,1,0:T(8,128)(2,1)} %copy-done) | copy-start | bytes 7864324

commit v6 on v4

--- a/solution.py
+++ b/solution.py
@@ -20,8 +20,9 @@
 BATCH = 8
 WIDE = BATCH * RANK
 SIDES = 4
-BY_LANE = 3
-FAR = 8
+BY_LANE = 2
+FAR = 16
+DOWN = 32
 EMPTY = 512
 SENT = RANK + 16
 f32 = jnp.float32
@@ -162,12 +163,12 @@
     def flush(q):
         pltpu.make_async_copy(send_ref.at[pl.ds(q, FAR)], send_any.at[pl.ds(q, FAR)], out_sem.at[1]).start()
 
-    gather_rows(table_ref, stack_ref, place_ref, group_ref, hot_ref, store, flush)
     select_ops(far_op_ref, near_op_ref, m2l_ref, copies[6].wait, far_ref, near_ref)
     near_out = pltpu.make_async_copy(near_ref, near_any, out_sem.at[2])
     far_out = pltpu.make_async_copy(far_ref, far_any, out_sem.at[3])
     near_out.start()
     far_out.start()
+    gather_rows(table_ref, stack_ref, place_ref, group_ref, hot_ref, store, flush)
     poles_out.wait()
     pltpu.make_async_copy(send_ref, send_any, out_sem.at[1]).wait()
     near_out.wait()
@@ -204,12 +205,17 @@
     )(child, source, target, flat, m2m, far_op.reshape(1, CAP), near_op.reshape(1, PAIRS))
 
 
-def serve_kernel(poles_ref, received_any, out_any, out_ref, ask_ref, in_sem, out_sem,
+def serve_kernel(poles_any, received_any, out_any, out_ref, ask_ref, in_sem, pole_sem, out_sem,
                  table_ref, stack_ref, place_ref, group_ref, hot_ref):
     asked = pltpu.make_async_copy(received_any.at[:, RANK:SENT, :], ask_ref, in_sem)
     asked.start()
+    poles = [pltpu.make_async_copy(poles_any.at[:, k * TB:(k + 1) * TB],
+                                   stack_ref.at[k * RANK:(k + 1) * RANK, :], pole_sem.at[k]) for k in range(NB)]
+    for copy in poles:
+        copy.start()
     fill_table(table_ref)
-    stack_groups(poles_ref, stack_ref)
+    for copy in poles:
+        copy.wait()
     asked.wait()
 
     def unpack(n, _):
@@ -235,12 +241,13 @@
     return pl.pallas_call(
         serve_kernel,
         out_shape=jax.ShapeDtypeStruct((PEERS, RANK, CAP), bf16),
-        in_specs=[VMEM, ANY],
+        in_specs=[ANY, ANY],
         out_specs=ANY,
         scratch_shapes=[
             pltpu.VMEM((PEERS, RANK, CAP), bf16),
             pltpu.VMEM((PEERS, SENT - RANK, CAP), bf16),
             pltpu.SemaphoreType.DMA,
+            pltpu.SemaphoreType.DMA((NB,)),
             pltpu.SemaphoreType.DMA,
         ] + GATHER_SCRATCH,
         compiler_params=pltpu.CompilerParams(vmem_limit_bytes=LIMIT),
@@ -344,11 +351,11 @@
                 served_ref, own_ref, out_ref, in_sem, out_sem,
                 table_ref, place_ref, group_ref, hot_ref, spread_ref, total_ref, local_ref):
     def fetch(n):
-        rows = pl.ds(n * FAR, FAR)
+        rows = pl.ds(n * DOWN, DOWN)
         return (pltpu.make_async_copy(served_any.at[rows], served_ref.at[rows], in_sem.at[0, n]),
                 pltpu.make_async_copy(own_any.at[rows], own_ref.at[rows], in_sem.at[1, n]))
 
-    for n in range(CAP // FAR):
+    for n in range(CAP // DOWN):
         for copy in fetch(n):
             copy.start()
     fill_table(table_ref)
@@ -358,13 +365,13 @@
     total_ref[...] = jnp.zeros(total_ref.shape, f32)
 
     def step(n, _):
-        at = pl.multiple_of(n * FAR, FAR)
+        at = pl.multiple_of(n * DOWN, DOWN)
         for copy in fetch(n):
             copy.wait()
-        source_places = place_ref[pl.ds(at, FAR), :]
-        source_groups = group_ref[pl.ds(at, FAR), :]
-
-        for i in range(0, FAR, 2):
+        source_places = place_ref[pl.ds(at, DOWN), :]
+        source_groups = group_ref[pl.ds(at, DOWN), :]
+
+        for i in range(0, DOWN, 2):
             back, ahead, places, groups = [], [], [], []
             for k in range(2):
                 c = at + i + k
@@ -383,7 +390,7 @@
         total_ref[...] += lax.dot_general(spread_ref[...], hot_ref[...], NT, preferred_element_type=f32)
         return 0
 
-    lax.fori_loop(0, CAP // FAR, step, 0)
+    lax.fori_loop(0, CAP // DOWN, step, 0)
     ops = jnp.concatenate([m2m_ref[c] for c in range(CHILD)], axis=1)
     for k in range(NB):
         cols = slice(k * TB, (k + 1) * TB)
@@ -407,13 +414,13 @@
             pltpu.VMEM(served.shape, bf16),
             pltpu.VMEM(own.shape, bf16),
             pltpu.VMEM((CHILD * RANK, BOX), bf16),
-            pltpu.SemaphoreType.DMA((2, CAP // FAR)),
+            pltpu.SemaphoreType.DMA((2, CAP // DOWN)),
             pltpu.SemaphoreType.DMA,
             pltpu.VMEM((TB, LANES), bf16),
             pltpu.VMEM((CAP, PEERS), f32),
             pltpu.VMEM((CAP, PEERS), f32),
-            pltpu.VMEM((TB, 2 * FAR * PEERS), bf16),
-            pltpu.VMEM((STACK, 2 * FAR * PEERS), bf16),
+            pltpu.VMEM((TB, 2 * DOWN * PEERS), bf16),
+            pltpu.VMEM((STACK, 2 * DOWN * PEERS), bf16),
             pltpu.VMEM((STACK, TB), f32),
             pltpu.VMEM((RANK, BOX), bf16),
         ],

time: 145 us -> 138 us (0.952)
  Pallas kernels: 113 us -> 105 us
    pallas_call x1, Pallas kernels: 20.5 us -> 17.2 us  [downward(): pl.pallas_call(down_kernel, out_shape=jax.ShapeDtypeStruct((CHILD * RANK,...]
    pallas_call x1, Pallas kernels: 9.91 us -> 7.88 us  [serve(): pl.pallas_call(serve_kernel, out_shape=jax.ShapeDtypeStruct((PEERS, RANK,...]
    pallas_call x1, Pallas kernels: 13.3 us -> 11.5 us  [upward(): pl.pallas_call(up_kernel, out_shape=out_shape, in_specs=[ANY] * 4 + [VMEM...]
  transfers between devices with their start and end apart: 2 -> 2, of which waited for: 0 -> 0; matrix products, arithmetic and copies ran while one was open for 3% -> 3% of each run, Pallas kernels for 48% -> 50%
where the time goes in v6:
time: 138 us; the launch traced here: 137 us
  Pallas kernels  105 us (76%)
  starting transfers between devices  21.7 us (16%)
  local copies, waits for them, and re-layouts  10 us (7%)
    pallas_call x2, Pallas kernels, near(): pl.pallas_call(functools.partial(near_kernel, first, batches), out_shape=...  68.7 us
    pallas_call x1, Pallas kernels, downward(): pl.pallas_call(down_kernel, out_shape=jax.ShapeDtypeStruct((CHILD * RANK,...  17.2 us
    all_to_all x1, starting transfers between devices, on_device(): lax.all_to_all(send, ('curve', 'sub'), split_axis=0, concat_axis=0, tiled...  11.5 us
    pallas_call x1, Pallas kernels, upward(): pl.pallas_call(up_kernel, out_shape=out_shape, in_specs=[ANY] * 4 + [VMEM...  11.5 us
    all_to_all x1, starting transfers between devices, on_device(): lax.all_to_all(answer, ('curve', 'sub'), split_axis=0, concat_axis=0, til...  10.2 us
    pallas_call x1, Pallas kernels, serve(): pl.pallas_call(serve_kernel, out_shape=jax.ShapeDtypeStruct((PEERS, RANK,...  7.88 us
    all_to_all x1, local copies, waits for them, and re-layouts, on_device(): lax.all_to_all(answer, ('curve', 'sub'), split_axis=0, concat_axis=0, til...  4.57 us
    all_to_all x1, local copies, waits for them, and re-layouts, on_device(): lax.all_to_all(send, ('curve', 'sub'), split_axis=0, concat_axis=0, tiled...  3.9 us
  transfers between devices with their start and end apart: 2, of which 0 were waited for; matrix products, arithmetic and copies ran while one was open for 3% of the time, Pallas kernels for 50%

profile of v6, /device:TPU:1, one launch (start us, length us, event | category | flops | bytes accessed | tf_op | source)
XLA Modules:
  0.0 137.3 jit_solution(8007658457965859255)
XLA Ops:
  0.0 11.5 %upward.1 = (bf16[64,2048]{1,0:T(8,128)(2,1)}, bf16[128,80,128]{2,1,0:T(8,128)(2,1)}, f32[4096,128]{1,0:T(8,128)}, f32[2816,128]{1,0:T(8,128)}) custom-call(bf16[512,2048]{1,0:T(8,128)(2,1)} %bitcast.14, s32[128,128]{1,0:T(8,128)} %bitcast.16, s32[128,128]{1,0:T(8,128)} %bitcast.15, bf16[4096,316]{1,0:T(8,128)(2,1)} %bitcast.13, bf16[8,64,64]{2,1,0:T(8,128)(2,1)} %m2m_ref.3, ...), custom_call_target="tpu_custom_call" | custom-call | flops 10000000000 | bytes 12582912 | tf_op jit(solution)/shard_map/upward/pallas_call | solution.py:186
  11.5 11.5 %all-to-all-start = ((bf16[128,80,128]{2,1,0:T(8,128)(2,1)}), bf16[128,80,128]{2,1,0:T(8,128)(2,1)S(1)}, u32[]{:S(2)}, u32[]{:S(2)}) async-start(bf16[128,80,128]{2,1,0:T(8,128)(2,1)} %get-tuple-element.10), calls=%async_computation | async-start | bytes 5242880 | tf_op jit(solution)/shard_map/all_to_all | solution.py:437
  23.0 37.2 %near.2.near_a_ref = f32[64,2048]{1,0:T(8,128)} custom-call(bf16[64,2048]{1,0:T(8,128)(2,1)} %get-tuple-element.9.poles_any.poles_ref, s32[88,2048]{1,0:T(8,128)} %partner_ref.3, f32[2816,128]{1,0:T(8,128)} %get-tuple-element.11.ops_ref), custom_call_target="tpu_custom_call" | custom-call | flops 48000000000 | bytes 6291456 | tf_op jit(solution)/shard_map/near/pallas_call | solution.py:326
  60.2 0.0 all-to-all-done.received_any
  60.2 0.0 copy-start
  60.2 1.5 %copy-done = bf16[128,80,128]{2,1,0:T(8,128)(2,1)} copy-done((bf16[128,80,128]{2,1,0:T(8,128)(2,1)}, bf16[128,80,128]{2,1,0:T(8,128)(2,1)S(1)}, u32[]{:S(2)}) %copy-start) | copy-done | bytes 2621464
  61.7 7.9 %serve.1 = bf16[128,64,128]{2,1,0:T(8,128)(2,1)} custom-call(bf16[64,2048]{1,0:T(8,128)(2,1)} %get-tuple-element.9.poles_any.poles_ref, bf16[128,80,128]{2,1,0:T(8,128)(2,1)} %copy-done), custom_call_target="tpu_custom_call" | custom-call | flops 10000000000 | bytes 4194304 | tf_op jit(solution)/shard_map/serve/pallas_call | solution.py:241
  69.6 10.2 %all-to-all-start.1 = ((bf16[128,64,128]{2,1,0:T(8,128)(2,1)}), bf16[128,64,128]{2,1,0:T(8,128)(2,1)}, u32[]{:S(2)}, u32[]{:S(2)}) async-start(bf16[128,64,128]{2,1,0:T(8,128)(2,1)} %serve.1), calls=%async_computation.1 | async-start | bytes 4194304 | tf_op jit(solution)/shard_map/all_to_all | solution.py:441
  79.8 0.0 copy-start.1
  79.8 31.6 %near.3.near_b_ref = f32[64,2048]{1,0:T(8,128)} custom-call(bf16[64,2048]{1,0:T(8,128)(2,1)} %get-tuple-element.9.poles_any.poles_ref, s32[88,2048]{1,0:T(8,128)} %partner_ref.3, f32[2816,128]{1,0:T(8,128)} %get-tuple-element.11.ops_ref), custom_call_target="tpu_custom_call" | custom-call | flops 40000000000 | bytes 6291456 | tf_op jit(solution)/shard_map/near/pallas_call | solution.py:326
  111.4 0.0 copy-done.1
  111.4 3.9 %copy.18 = bf16[128,80,128]{0,1,2:T(8,128)(2,1)} copy(bf16[128,80,128]{2,1,0:T(8,128)(2,1)S(1)} %copy-done.1) | data formatting | bytes 5242880 | tf_op jit(solution)/shard_map/all_to_all | solution.py:437
  115.3 0.0 all-to-all-done.1
  115.3 4.6 %copy.17 = bf16[128,64,128]{0,1,2:T(8,128)(2,1)} copy(bf16[128,64,128]{2,1,0:T(8,128)(2,1)} %all-to-all-done.1) | data formatting | bytes 4194304 | tf_op jit(solution)/shard_map/all_to_all | solution.py:441
  119.9 17.2 %downward.1 = bf16[512,2048]{1,0:T(8,128)(2,1)} custom-call(bf16[128,64,128]{2,1,0:T(8,128)(2,1)} %bitcast.12, bf16[128,80,128]{2,1,0:T(8,128)(2,1)} %bitcast.11, f32[64,2048]{1,0:T(8,128)} %near.2.near_a_ref, f32[64,2048]{1,0:T(8,128)} %near.3.near_b_ref, s32[128,128]{1,0:T(8,128)} %bitcast.17, f32[4096,128]{1,0:T(8,128)} %get-tuple-element.12.ops_ref, ...), custom_call_target="tpu_custom_call" | custom-call | flops 20000000000 | bytes 16777216 | tf_op jit(solution)/shard_map/downward/pallas_call | solution.py:408
Async XLA Ops:
  11.5 48.7 %all-to-all-start = ((bf16[128,80,128]{2,1,0:T(8,128)(2,1)}), bf16[128,80,128]{2,1,0:T(8,128)(2,1)S(1)}, u32[]{:S(2)}, u32[]{:S(2)}) async-start(bf16[128,80,128]{2,1,0:T(8,128)(2,1)} %get-tuple-element.10), calls=%async_computation | async-start | bytes 5242880 | tf_op jit(solution)/shard_map/all_to_all | solution.py:437
  60.2 1.5 %copy-start = (bf16[128,80,128]{2,1,0:T(8,128)(2,1)}, bf16[128,80,128]{2,1,0:T(8,128)(2,1)S(1)}, u32[]{:S(2)}) copy-start(bf16[128,80,128]{2,1,0:T(8,128)(2,1)S(1)} %all-to-all-done.received_any) | copy-start | bytes 7864324
  69.6 45.7 %all-to-all-start.1 = ((bf16[128,64,128]{2,1,0:T(8,128)(2,1)}), bf16[128,64,128]{2,1,0:T(8,128)(2,1)}, u32[]{:S(2)}, u32[]{:S(2)}) async-start(bf16[128,64,128]{2,1,0:T(8,128)(2,1)} %serve.1), calls=%async_computation.1 | async-start | bytes 4194304 | tf_op jit(solution)/shard_map/all_to_all | solution.py:441
  79.8 31.6 %copy-start.1 = (bf16[128,80,128]{2,1,0:T(8,128)(2,1)S(1)}, bf16[128,80,128]{2,1,0:T(8,128)(2,1)}, u32[]{:S(2)}) copy-start(bf16[128,80,128]{2,1,0:T(8,128)(2,1)} %copy-done) | copy-start | bytes 7864324
